TPU v7x, 32 devices: a whole 2x2x4 slice. The times are simulated.
32 devices in a mesh: dp: 4 (over y, core), row: 2 (over x), col: 4 (over z).
Axes of the slice: x: 2, y: 2, z: 4, core: 2. Of those that a mesh axis runs over, the one named last changes fastest.
Arguments:
- tokens: bfloat16 [3072, 4096], P('dp', ('row', 'col')), may hold values from -6 to 6
- cotangent: bfloat16 [3072, 4096], P('dp', ('row', 'col')), may hold values from -4 to 4
- gate_weight: bfloat16 [4096, 14336], P('row', 'col'), may hold values from -0.09375 to 0.09375
- up_weight: bfloat16 [4096, 14336], P('row', 'col'), may hold values from -0.09375 to 0.09375
- down_weight: bfloat16 [14336, 4096], P('col', 'row'), may hold values from -0.046875 to 0.046875
Outputs:
- layer_out: bfloat16 [3072, 4096], P(('dp', 'col'), 'row')
- input_grad: bfloat16 [3072, 4096], P(('dp', 'col'), 'row')
- gate_wgrad: bfloat16 [4096, 14336], P('row', 'col')
- up_wgrad: bfloat16 [4096, 14336], P('row', 'col')
- down_wgrad: bfloat16 [14336, 4096], P('col', 'row')
All inputs are finite; a program needn't handle non-finite values.
Results may differ from a plain program's by a relative error of at most 0.034.
Values may be sent and summed in bfloat16 or wider, within the bound.
A program may use at most 256 MiB of HBM per device.

v0:
```python
import jax
import jax.numpy as jnp
from jax import lax
from jax.sharding import PartitionSpec as P


def contract_rows(left, right):
    return lax.dot_general(
        left, right, (((0,), (0,)), ((), ())), preferred_element_type=jnp.float32
    )


def contract_cols(left, right):
    return lax.dot_general(
        left, right, (((1,), (1,)), ((), ())), preferred_element_type=jnp.float32
    )


def local(tokens, cotangent, gate_weight, up_weight, down_weight):
    f32 = jnp.float32
    whole_x, whole_dy = (
        lax.all_gather(tokens, "col", axis=1, tiled=True),
        lax.all_gather(cotangent, "col", axis=1, tiled=True),
    )
    width = gate_weight.shape[1]
    rows = whole_x
    stacked = lax.psum_scatter(
        jnp.concatenate(
            [
                jnp.dot(rows, gate_weight, preferred_element_type=f32),
                jnp.dot(rows, up_weight, preferred_element_type=f32),
            ],
            axis=1,
        ).astype(jnp.bfloat16),
        "row",
        scatter_dimension=0,
        tiled=True,
    ).astype(jnp.float32)
    gate = stacked[:, :width]
    up = stacked[:, width:]
    sigma = jax.nn.sigmoid(gate)
    silu_gate = gate * sigma
    hidden = (silu_gate * up).astype(jnp.bfloat16)
    hidden_all = lax.all_gather(hidden, "row", axis=0, tiled=True)
    out_terms = jnp.dot(hidden_all, down_weight, preferred_element_type=f32)
    layer_out = lax.psum_scatter(
        out_terms.astype(jnp.bfloat16), "col", scatter_dimension=0, tiled=True
    )
    down_part = contract_rows(hidden_all, whole_dy).astype(jnp.bfloat16)
    rows = whole_dy
    hidden_grad = lax.psum_scatter(
        contract_cols(rows, down_weight).astype(jnp.bfloat16),
        "row",
        scatter_dimension=0,
        tiled=True,
    ).astype(jnp.float32)
    gate_grad = (hidden_grad * up * sigma * (1.0 + gate * (1.0 - sigma))).astype(jnp.bfloat16)
    up_grad = (hidden_grad * silu_gate).astype(jnp.bfloat16)
    gate_all, up_all = (
        lax.all_gather(gate_grad, "row", axis=0, tiled=True),
        lax.all_gather(up_grad, "row", axis=0, tiled=True),
    )
    input_grad = lax.psum_scatter(
        (contract_cols(gate_all, gate_weight) + contract_cols(up_all, up_weight)).astype(
            jnp.bfloat16
        ),
        "col",
        scatter_dimension=0,
        tiled=True,
    )
    gate_part = contract_rows(whole_x, gate_all).astype(jnp.bfloat16)
    up_part = contract_rows(whole_x, up_all).astype(jnp.bfloat16)
    gate_sum, up_sum, down_sum = (
        lax.psum(gate_part.astype(f32).astype(jnp.bfloat16), "dp").astype(jnp.float32),
        lax.psum(up_part.astype(f32).astype(jnp.bfloat16), "dp").astype(jnp.float32),
        lax.psum(down_part.astype(f32).astype(jnp.bfloat16), "dp").astype(jnp.float32),
    )
    gate_wgrad = gate_sum.astype(jnp.bfloat16)
    up_wgrad = up_sum.astype(jnp.bfloat16)
    down_wgrad = down_sum.astype(jnp.bfloat16)
    return (layer_out, input_grad, gate_wgrad, up_wgrad, down_wgrad)


def solution(mesh):
    in_specs = (
        P("dp", ("row", "col")),
        P("dp", ("row", "col")),
        P("row", "col"),
        P("row", "col"),
        P("col", "row"),
    )
    out_specs = (
        P(("dp", "col"), "row"),
        P(("dp", "col"), "row"),
        P("row", "col"),
        P("row", "col"),
        P("col", "row"),
    )
    return jax.shard_map(local, mesh=mesh, in_specs=in_specs, out_specs=out_specs, check_vma=False)
```

profile of v0, /device:TPU:0, one launch (start us, length us, event | category | flops | bytes accessed | tf_op | source)
XLA Modules:
  0.0 1459.6 jit_solution(7137696746744348982)
XLA Ops:
  7.2 0.0 all-gather.6.cloned.1.call-start
  7.2 0.7 all-gather.6.cloned.1.call-update
  7.9 0.0 all-gather.10.cloned.1.call-start
  7.9 0.7 all-gather.10.cloned.1.call-update
  8.6 0.0 reduce-scatter.5.cloned.1.call-start
  8.7 67.1 %all-gather.6.cloned.1.call-done = bf16[768,2048]{1,0:T(8,128)(2,1)} async-done(((bf16[768,512]{1,0:T(8,128)(2,1)}), bf16[768,2048]{1,0:T(8,128)(2,1)}) %all-gather.6.cloned.1.call-update) | async-done | bytes 3145744 | tf_op jit(solution)/shard_map/all_gather | solution.py:22
  75.8 0.0 copy-start
  75.8 17.6 %convolution_convert_fusion.4 = bf16[768,3584]{1,0:T(8,128)(2,1)S(1)} fusion(bf16[768,2048]{1,0:T(8,128)(2,1)} %all-gather.6.cloned.1.call-done, bf16[2048,3584]{1,0:T(8,128)(2,1)} %param.8), kind=kOutput, calls=%fused_computation.9 | convolution fusion | flops 11277041664 | bytes 23330816 | tf_op jit(solution)/shard_map/dot_general | solution.py:31
  93.4 0.0 copy-done
  93.4 14.9 %convolution_convert_fusion.5 = bf16[768,3584]{1,0:T(8,128)(2,1)S(1)} fusion(bf16[768,2048]{1,0:T(8,128)(2,1)S(1)} %copy-done, bf16[2048,3584]{1,0:T(8,128)(2,1)} %param.7), kind=kOutput, calls=%fused_computation.10 | convolution fusion | flops 11277041664 | bytes 23330816 | tf_op jit(solution)/shard_map/dot_general | solution.py:30
  108.3 4.9 pad_maximum_fusion
  113.2 0.0 reduce-scatter.5.cloned.1.call-update
  113.2 0.2 reduce-scatter.9.cloned.1.call-start
  113.4 26.1 %all-gather.10.cloned.1.call-done = bf16[768,2048]{1,0:T(8,128)(2,1)} async-done(((bf16[768,512]{1,0:T(8,128)(2,1)}), bf16[768,2048]{1,0:T(8,128)(2,1)}) %all-gather.10.cloned.1.call-update) | async-done | bytes 3145744 | tf_op jit(solution)/shard_map/all_gather | solution.py:23
  139.5 17.3 %convolution_convert_fusion.3 = bf16[768,3584]{1,0:T(8,128)(2,1)} fusion(bf16[768,2048]{1,0:T(8,128)(2,1)} %all-gather.10.cloned.1.call-done, bf16[3584,2048]{1,0:T(8,128)(2,1)} %param.9), kind=kOutput, calls=%fused_computation.8 | convolution fusion | flops 11277041664 | bytes 23330816 | tf_op jit(solution)/shard_map/dot_general | solution.py:14
  156.8 0.0 reduce-scatter.9.cloned.1.call-update
  156.8 0.0 all-gather.8.cloned.1.call-start
  156.9 111.7 %reduce-scatter.5.cloned.1.call-done = bf16[384,7168]{1,0:T(8,128)(2,1)} async-done(((bf16[768,7168]{1,0:T(8,128)(2,1)}), bf16[384,7168]{1,0:T(8,128)(2,1)}) %reduce-scatter.5.cloned.1.call-update) | async-done | bytes 5505040 | tf_op jit(solution)/shard_map/reduce_scatter | solution.py:27
  268.6 8.2 convert_element_type.52
  276.8 63.1 %reduce-scatter.9.cloned.1.call-done = bf16[384,3584]{1,0:T(8,128)(2,1)} async-done(((bf16[768,3584]{1,0:T(8,128)(2,1)}), bf16[384,3584]{1,0:T(8,128)(2,1)}) %reduce-scatter.9.cloned.1.call-update) | async-done | bytes 2752528 | tf_op jit(solution)/shard_map/reduce_scatter | solution.py:51
  339.9 8.6 fusion.5
  348.5 0.0 all-gather.8.cloned.1.call-update
  348.6 0.0 all-gather.14.cloned.1.call-start
  348.6 0.5 all-gather.14.cloned.1.call-update
  349.1 0.0 all-gather.12.cloned.1.call-start
  349.2 0.7 all-gather.12.cloned.1.call-update
  349.9 0.3 all-reduce.3.cloned.1.call-start
  350.1 70.1 %all-gather.8.cloned.1.call-done = bf16[768,3584]{1,0:T(8,128)(2,1)} async-done(((bf16[384,3584]{1,0:T(8,128)(2,1)}), bf16[768,3584]{1,0:T(8,128)(2,1)}) %all-gather.8.cloned.1.call-update) | async-done | bytes 5505040 | tf_op jit(solution)/shard_map/all_gather | solution.py:44
  420.2 17.6 %convolution_convert_fusion = bf16[3584,2048]{1,0:T(8,128)(2,1)} fusion(bf16[768,3584]{1,0:T(8,128)(2,1)} %all-gather.8.cloned.1.call-done, bf16[768,2048]{1,0:T(8,128)(2,1)} %all-gather.10.cloned.1.call-done), kind=kOutput, calls=%fused_computation | convolution fusion | flops 11281629184 | bytes 23330816 | tf_op jit(solution)/shard_map/dot_general | solution.py:8
  437.9 55.9 %all-gather.14.cloned.1.call-done = bf16[768,3584]{1,0:T(8,128)(2,1)} async-done(((bf16[384,3584]{1,0:T(8,128)(2,1)}), bf16[768,3584]{1,0:T(8,128)(2,1)}) %all-gather.14.cloned.1.call-update) | async-done | bytes 5505040 | tf_op jit(solution)/shard_map/all_gather | solution.py:61
  493.8 16.7 %fusion.1 = bf16[2048,3584]{0,1:T(8,128)(2,1)} fusion(bf16[768,3584]{1,0:T(8,128)(2,1)} %all-gather.14.cloned.1.call-done, bf16[768,2048]{1,0:T(8,128)(2,1)S(1)} %copy-done), kind=kOutput, calls=%fused_computation.4 | convolution fusion | flops 11281629184 | bytes 23330816 | tf_op jit(solution)/shard_map/dot_general | solution.py:8
  510.5 56.5 %all-gather.12.cloned.1.call-done = bf16[768,3584]{1,0:T(8,128)(2,1)} async-done(((bf16[384,3584]{1,0:T(8,128)(2,1)}), bf16[768,3584]{1,0:T(8,128)(2,1)}) %all-gather.12.cloned.1.call-update) | async-done | bytes 5505040 | tf_op jit(solution)/shard_map/all_gather | solution.py:60
  567.0 16.7 %fusion = bf16[2048,3584]{0,1:T(8,128)(2,1)} fusion(bf16[768,3584]{1,0:T(8,128)(2,1)} %all-gather.12.cloned.1.call-done, bf16[768,2048]{1,0:T(8,128)(2,1)S(1)} %copy-done), kind=kOutput, calls=%fused_computation.3 | convolution fusion | flops 11281629184 | bytes 23330816 | tf_op jit(solution)/shard_map/dot_general | solution.py:8
  583.6 0.0 all-reduce.3.cloned.1.call-update
  583.7 0.3 reduce-scatter.7.cloned.1.call-start
  584.0 17.5 %convolution_convert_fusion.6 = bf16[768,2048]{1,0:T(8,128)(2,1)} fusion(bf16[768,3584]{1,0:T(8,128)(2,1)} %all-gather.8.cloned.1.call-done, bf16[3584,2048]{1,0:T(8,128)(2,1)} %param.9), kind=kOutput, calls=%fused_computation.19 | convolution fusion | flops 11275862016 | bytes 23330816 | tf_op jit(solution)/shard_map/dot_general | solution.py:45
  601.5 0.0 reduce-scatter.7.cloned.1.call-update
  601.5 0.0 reduce-scatter.11.cloned.1.call-start
  601.6 16.6 %fusion.7 = f32[768,2048]{1,0:T(8,128)S(1)} fusion(bf16[768,3584]{1,0:T(8,128)(2,1)} %all-gather.12.cloned.1.call-done, bf16[2048,3584]{1,0:T(8,128)(2,1)} %param.7), kind=kOutput, calls=%fused_computation.20 | convolution fusion | flops 11274289152 | bytes 26476544 | tf_op jit(solution)/shard_map/dot_general | solution.py:14
  618.2 17.7 %add_convert_fusion = bf16[768,2048]{1,0:T(8,128)(2,1)} fusion(f32[768,2048]{1,0:T(8,128)S(1)} %fusion.7, bf16[768,3584]{1,0:T(8,128)(2,1)} %all-gather.14.cloned.1.call-done, bf16[2048,3584]{1,0:T(8,128)(2,1)} %param.8), kind=kOutput, calls=%fused_computation.11 | convolution fusion | flops 11277434880 | bytes 29622272 | tf_op jit(solution)/shard_map/dot_general | solution.py:14
  635.9 0.0 reduce-scatter.11.cloned.1.call-update
  635.9 676.5 %all-reduce.3.cloned.1.call-done = (bf16[2048,3584]{0,1:T(8,128)(2,1)}, bf16[2048,3584]{0,1:T(8,128)(2,1)}, bf16[3584,2048]{1,0:T(8,128)(2,1)}) async-done(((bf16[2048,3584]{0,1:T(8,128)(2,1)}, bf16[2048,3584]{0,1:T(8,128)(2,1)}, bf16[3584,2048]{1,0:T(8,128)(2,1)}), (bf16[2048,3584]{0,1:T(8,128)(2,1)}, bf16[2048,3584]{0,1:T(8,128)(2,1)}, bf16[3584,2048]{1,0:T(8,128)(2,1)})) %all-reduce.3.cloned.1.call-update) | async-done | bytes 44040208 | tf_op jit(solution)/shard_map/psum | solution.py:74
  1312.4 19.1 %copy.10 = bf16[2048,3584]{1,0:T(8,128)(2,1)} copy(bf16[2048,3584]{0,1:T(8,128)(2,1)} %get-tuple-element.10) | data formatting | bytes 29360128
  1331.5 18.7 %copy.11 = bf16[2048,3584]{1,0:T(8,128)(2,1)} copy(bf16[2048,3584]{0,1:T(8,128)(2,1)} %get-tuple-element.11) | data formatting | bytes 29360128
  1350.2 25.6 %reduce-scatter.7.cloned.1.call-done = bf16[192,2048]{1,0:T(8,128)(2,1)} async-done(((bf16[768,2048]{1,0:T(8,128)(2,1)}), bf16[192,2048]{1,0:T(8,128)(2,1)}) %reduce-scatter.7.cloned.1.call-update) | async-done | bytes 786448 | tf_op jit(solution)/shard_map/reduce_scatter | solution.py:46
  1375.8 63.0 %reduce-scatter.11.cloned.1.call-done = bf16[192,2048]{1,0:T(8,128)(2,1)} async-done(((bf16[768,2048]{1,0:T(8,128)(2,1)}), bf16[192,2048]{1,0:T(8,128)(2,1)}) %reduce-scatter.11.cloned.1.call-update) | async-done | bytes 786448 | tf_op jit(solution)/shard_map/reduce_scatter | solution.py:63
  1438.8 13.5 copy.15
Async XLA Ops:
  7.2 68.6 %all-gather.6.cloned.1.call-start = ((), (), s32[]{:S(2)}) async-start(), calls=%async_computation.4 | async-start | bytes 3932160 | tf_op jit(solution)/shard_map/all_gather | solution.py:22
  7.9 131.6 %all-gather.10.cloned.1.call-start = ((), (), s32[]{:S(2)}) async-start(), calls=%async_computation.8 | async-start | bytes 3932160 | tf_op jit(solution)/shard_map/all_gather | solution.py:23
  8.6 260.0 %reduce-scatter.5.cloned.1.call-start = ((), (), s32[]{:S(2)}) async-start(), calls=%async_computation.5 | async-start | bytes 16515072 | tf_op jit(solution)/shard_map/reduce_scatter | solution.py:27
  75.8 17.6 %copy-start = (bf16[768,2048]{1,0:T(8,128)(2,1)S(1)}, bf16[768,2048]{1,0:T(8,128)(2,1)}, u32[]{:S(2)}) copy-start(bf16[768,2048]{1,0:T(8,128)(2,1)} %all-gather.6.cloned.1.call-done) | copy-start | bytes 9437188
  113.2 226.7 %reduce-scatter.9.cloned.1.call-start = ((), (), s32[]{:S(2)}) async-start(), calls=%async_computation.9 | async-start | bytes 8257536 | tf_op jit(solution)/shard_map/reduce_scatter | solution.py:51
  156.8 263.4 %all-gather.8.cloned.1.call-start = ((), (), s32[]{:S(2)}) async-start(), calls=%async_computation.6 | async-start | bytes 8257536 | tf_op jit(solution)/shard_map/all_gather | solution.py:44
  348.6 145.3 %all-gather.14.cloned.1.call-start = ((), (), s32[]{:S(2)}) async-start(), calls=%async_computation.11 | async-start | bytes 8257536 | tf_op jit(solution)/shard_map/all_gather | solution.py:61
  349.1 217.9 %all-gather.12.cloned.1.call-start = ((), (), s32[]{:S(2)}) async-start(), calls=%async_computation.10 | async-start | bytes 8257536 | tf_op jit(solution)/shard_map/all_gather | solution.py:60
  349.9 962.5 %all-reduce.3.cloned.1.call-start = ((), (), s32[]{:S(2)}) async-start(), calls=%async_computation.13 | async-start | bytes 88080384 | tf_op jit(solution)/shard_map/psum | solution.py:74
  583.7 792.1 %reduce-scatter.7.cloned.1.call-start = ((), (), s32[]{:S(2)}) async-start(), calls=%async_computation.7 | async-start | bytes 3932160 | tf_op jit(solution)/shard_map/reduce_scatter | solution.py:46
  601.5 837.3 %reduce-scatter.11.cloned.1.call-start = ((), (), s32[]{:S(2)}) async-start(), calls=%async_computation.12 | async-start | bytes 3932160 | tf_op jit(solution)/shard_map/reduce_scatter | solution.py:63
Sparse Core Ops, SparseCore 0:
  9.6 66.1 all-gather.5
  77.3 62.1 all-gather.9
  142.4 126.1 reduce-scatter.4
  271.3 68.5 reduce-scatter.8
  348.7 71.5 all-gather.7
  422.3 71.5 all-gather.13
  495.4 71.5 all-gather.11
  583.8 728.5 all-reduce.2
  1315.3 60.4 reduce-scatter.6
  1378.5 60.2 reduce-scatter.10
where the time goes:
time: 1470 us; the launch traced here: 1460 us
  waiting for transfers between devices  1220 us (83%)
  matrix products  153 us (10%)
  local copies, waits for them, and re-layouts  51.3 us (3%)
  other arithmetic  21.7 us (1%)
    psum x1, waiting for transfers between devices, local(): lax.psum(gate_part.astype(f32).astype(jnp.bfloat16), 'dp')  676 us
    reduce_scatter x1, waiting for transfers between devices, local(): lax.psum_scatter(jnp.concatenate([jnp.dot(rows, gate_weight, preferred_el...  112 us
    all_gather x1, waiting for transfers between devices, local(): hidden_all = lax.all_gather(hidden, 'row', axis=0, tiled=True)  70.1 us
    all_gather x1, waiting for transfers between devices, local(): lax.all_gather(tokens, 'col', axis=1, tiled=True)  67.1 us
    reduce_scatter x1, waiting for transfers between devices, local(): lax.psum_scatter(contract_cols(rows, down_weight).astype(jnp.bfloat16), '...  63.1 us
    reduce_scatter x1, waiting for transfers between devices, local(): lax.psum_scatter((contract_cols(gate_all, gate_weight) + contract_cols(up...  63 us
    all_gather x1, waiting for transfers between devices, local(): lax.all_gather(gate_grad, 'row', axis=0, tiled=True)  56.5 us
    all_gather x1, waiting for transfers between devices, local(): lax.all_gather(up_grad, 'row', axis=0, tiled=True)  55.9 us
  transfers between devices with their start and end apart: 10, of which 10 were waited for; matrix products, arithmetic and copies ran while one was open for 13% of the time, Pallas kernels for 0%

commit v1 on v0

--- a/solution.py
+++ b/solution.py
@@ -1,7 +1,13 @@
+import functools
+
 import jax
 import jax.numpy as jnp
 from jax import lax
+from jax.experimental import pallas as pl
+from jax.experimental.pallas import tpu as pltpu
 from jax.sharding import PartitionSpec as P
+
+LANES = 128
 
 
 def contract_rows(left, right):
@@ -14,6 +20,177 @@
     return lax.dot_general(
         left, right, (((1,), (1,)), ((), ())), preferred_element_type=jnp.float32
     )
+
+
+def place_body(parts, outs, aliased, pos_ref, *refs):
+    ins = refs[: parts * outs]
+    results = refs[parts * outs + aliased :]
+    step = pl.program_id(0)
+    for part in range(parts):
+
+        @pl.when(step == part)
+        def _(part=part):
+            for out in range(outs):
+                results[out][...] = ins[part * outs + out][...]
+
+
+def place(pos, pieces, previous, total, offset, width, outs, axis):
+    parts = len(pieces)
+    steps = width // LANES
+    other = pieces[0].shape[1 - axis]
+    units = parts * total
+
+    def at(index):
+        return (index, 0) if axis == 0 else (0, index)
+
+    block = (LANES, other) if axis == 0 else (other, LANES)
+
+    def in_spec(part, out):
+        def index(j, i, pos_ref):
+            own = jnp.where(j == part, i, jnp.where(j < part, 0, steps - 1))
+            return at(out * steps + own)
+
+        return pl.BlockSpec(block, index)
+
+    def out_index(j, i, pos_ref):
+        return at(pos_ref[j] * (total // LANES) + offset // LANES + i)
+
+    shape = (units, other) if axis == 0 else (other, units)
+    operands = [pieces[part] for part in range(parts) for _ in range(outs)]
+    in_specs = [in_spec(part, out) for part in range(parts) for out in range(outs)]
+    aliases = {}
+    if previous is not None:
+        for out in range(outs):
+            aliases[1 + len(operands)] = out
+            operands.append(previous[out])
+            in_specs.append(pl.BlockSpec(memory_space=pl.ANY))
+    moved = 4 * parts * outs * width * other
+    return pl.pallas_call(
+        functools.partial(place_body, parts, outs, 0 if previous is None else outs),
+        out_shape=[jax.ShapeDtypeStruct(shape, jnp.bfloat16)] * outs,
+        grid_spec=pltpu.PrefetchScalarGridSpec(
+            num_scalar_prefetch=1,
+            grid=(parts, steps),
+            in_specs=in_specs,
+            out_specs=[pl.BlockSpec(block, out_index)] * outs,
+        ),
+        input_output_aliases=aliases,
+        compiler_params=pltpu.CompilerParams(vmem_limit_bytes=32 * 2**20),
+        cost_estimate=pl.CostEstimate(flops=0, bytes_accessed=moved, transcendentals=0),
+    )(pos, *operands)
+
+
+def local_units(tokens, cotangent, gate_weight, up_weight, down_weight):
+    f32, bf16 = jnp.float32, jnp.bfloat16
+    me = lax.axis_index("dp")
+    total = gate_weight.shape[1] // 4
+    first = -(-total // 512) * 256
+    bands = ((0, first), (first, total - first))
+    rows = tokens.shape[0]
+
+    def swap_row(a):
+        return lax.ppermute(a, "row", [(0, 1), (1, 0)])
+
+    def swap_core(a):
+        return lax.ppermute(a, "dp", [(i, i ^ 1) for i in range(4)])
+
+    def swap_y(a):
+        return lax.ppermute(a, "dp", [(i, i ^ 2) for i in range(4)])
+
+    start = me * total
+    gate_w = lax.dynamic_slice_in_dim(gate_weight, start, total, 1)
+    up_w = lax.dynamic_slice_in_dim(up_weight, start, total, 1)
+    down_w = lax.dynamic_slice_in_dim(down_weight, start, total, 0)
+    gu_w = [jnp.concatenate([gate_w[:, o : o + w], up_w[:, o : o + w]], axis=1) for o, w in bands]
+    d_w = [down_w[o : o + w] for o, w in bands]
+
+    x0 = lax.all_gather(tokens, "col", axis=1, tiled=True)
+    x2 = swap_y(x0)
+    x1, x3 = swap_core(x0), swap_core(x2)
+    dy0 = lax.all_gather(cotangent, "col", axis=1, tiled=True)
+    dy2 = swap_y(dy0)
+    dy1, dy3 = swap_core(dy0), swap_core(dy2)
+    x = [jnp.concatenate([x0, x1], axis=0), jnp.concatenate([x2, x3], axis=0)]
+    dy = [jnp.concatenate([dy0, dy1], axis=0), jnp.concatenate([dy2, dy3], axis=0)]
+
+    def forward(a, w):
+        mine = jnp.dot(a, w, preferred_element_type=f32).astype(bf16)
+        return mine, swap_row(mine)
+
+    gu = [[None, None], [None, None]]
+    early = [forward(x0, gu_w[0]), forward(x1, gu_w[0])]
+    gu[0][0] = tuple(jnp.concatenate([early[0][i], early[1][i]], axis=0) for i in range(2))
+    gu[0][1] = forward(x[1], gu_w[0])
+    gu[1][0] = forward(x[0], gu_w[1])
+    gu[1][1] = forward(x[1], gu_w[1])
+
+    def gates(band, half):
+        mine, theirs = gu[band][half]
+        both = mine.astype(f32) + theirs.astype(f32)
+        w = bands[band][1]
+        gate, up = both[:, :w], both[:, w:]
+        return gate, up, jax.nn.sigmoid(gate)
+
+    hidden = [[None, None], [None, None]]
+    for band in range(2):
+        for half in range(2):
+            gate, up, sigma = gates(band, half)
+            hidden[band][half] = (gate * sigma * up).astype(bf16)
+
+    def reduce_groups(halves):
+        sums = [
+            (a[:rows].astype(f32) + swap_core(a[rows:]).astype(f32)).astype(bf16) for a in halves
+        ]
+        far = lax.psum_scatter(sums[1], "col", scatter_dimension=0, tiled=True)
+        near = lax.psum_scatter(sums[0], "col", scatter_dimension=0, tiled=True)
+        return (near.astype(f32) + swap_y(far).astype(f32)).astype(bf16)
+
+    layer_out = reduce_groups(
+        [
+            jnp.dot(
+                jnp.concatenate([hidden[0][half], hidden[1][half]], axis=1),
+                down_w,
+                preferred_element_type=f32,
+            ).astype(bf16)
+            for half in range(2)
+        ]
+    )
+
+    def spread(a):
+        far = swap_y(a)
+        return [a, swap_core(a), far, swap_core(far)]
+
+    pos = jnp.stack([me, me ^ 1, me ^ 2, me ^ 3]).astype(jnp.int32)
+    down_wgrad, gu_wgrad = None, None
+    for band in range(2):
+        o, w = bands[band]
+        part = contract_rows(hidden[band][0], dy[0]) + contract_rows(hidden[band][1], dy[1])
+        down_wgrad = place(pos, spread(part.astype(bf16)), down_wgrad, total, o, w, 1, 0)
+
+    grads = [[None, None], [None, None]]
+    for band in range(2):
+        o, w = bands[band]
+        for half in (1, 0):
+            mine = contract_cols(dy[half], d_w[band]).astype(bf16)
+            hidden_grad = mine.astype(f32) + swap_row(mine).astype(f32)
+            gate, up, sigma = gates(band, half)
+            gate_grad = hidden_grad * up * sigma * (1.0 + gate * (1.0 - sigma))
+            up_grad = hidden_grad * (gate * sigma)
+            grads[band][half] = jnp.concatenate(
+                [gate_grad.astype(bf16), up_grad.astype(bf16)], axis=1
+            )
+        part = contract_rows(x[0], grads[band][0]) + contract_rows(x[1], grads[band][1])
+        gu_wgrad = place(pos, spread(part.astype(bf16)), gu_wgrad, total, o, w, 2, 1)
+
+    input_grad = reduce_groups(
+        [
+            (
+                contract_cols(grads[0][half], gu_w[0]) + contract_cols(grads[1][half], gu_w[1])
+            ).astype(bf16)
+            for half in range(2)
+        ]
+    )
+    return layer_out, input_grad, gu_wgrad[0], gu_wgrad[1], down_wgrad[0]
 
 
 def local(tokens, cotangent, gate_weight, up_weight, down_weight):
@@ -96,4 +273,17 @@
         P("row", "col"),
         P("col", "row"),
     )
-    return jax.shard_map(local, mesh=mesh, in_specs=in_specs, out_specs=out_specs, check_vma=False)
+    n_dp, n_row, n_col = (mesh.shape[name] for name in ("dp", "row", "col"))
+
+    def run(tokens, cotangent, gate_weight, up_weight, down_weight):
+        units = gate_weight.shape[1] // (n_col * n_dp)
+        split = n_dp == 4 and n_row == 2 and units % LANES == 0 and units >= 3 * LANES
+        return jax.shard_map(
+            local_units if split else local,
+            mesh=mesh,
+            in_specs=in_specs,
+            out_specs=out_specs,
+            check_vma=False,
+        )(tokens, cotangent, gate_weight, up_weight, down_weight)
+
+    return run

time: 1470 us -> 1020 us (0.69)
  waiting for transfers between devices: 1220 us -> 658 us
  Pallas kernels: 0 us -> 52.4 us
  matrix products: 153 us -> 181 us
  other arithmetic: 21.7 us -> 44.2 us
  starting transfers between devices: 1.04 us -> 21.3 us
    psum x1 -> x0, waiting for transfers between devices: 676 us -> none  [local(): lax.psum(gate_part.astype(f32).astype(jnp.bfloat16), 'dp')]
    ppermute x0 -> x33, waiting for transfers between devices: none -> 526 us  [the longest x8 314 us: swap_y(): return lax.ppermute(a, 'dp', [(i, i ^ 2) for i in range(4)])]
    reduce_scatter x4, waiting for transfers between devices: 263 us -> 0.01 us  [the longest x2 0.01 us: reduce_groups(): far = lax.psum_scatter(sums[1], 'col', scatter_dimension=0, tiled=True)]
    all_gather x5 -> x2, waiting for transfers between devices: 276 us -> 131 us  [the longest x1 67.1 us: local_units(): x0 = lax.all_gather(tokens, 'col', axis=1, tiled=True)]
    pallas_call x0 -> x4, Pallas kernels: none -> 52.4 us  [place(): pl.pallas_call(functools.partial(place_body, parts, outs, 0 if previous i...]
    unnamed x5 -> x120, local copies, waits for them, and re-layouts: 51.3 us -> 22.1 us
    ppermute x0 -> x33, starting transfers between devices: none -> 21.1 us  [the longest x9 10.8 us: swap_row(): return lax.ppermute(a, 'row', [(0, 1), (1, 0)])]
    convert_element_type x2 -> x10, other arithmetic: 16.8 us -> 37.1 us  [the longest x4 16.2 us: local_units(): gate_grad.astype(bf16)]
  transfers between devices with their start and end apart: 10 -> 39, of which waited for: 10 -> 13; matrix products, arithmetic and copies ran while one was open for 13% -> 25% of each run, Pallas kernels for 0% -> 5%
where the time goes in v1:
time: 1020 us; the launch traced here: 1010 us
  waiting for transfers between devices  658 us (65%)
  matrix products  181 us (18%)
  Pallas kernels  52.4 us (5%)
  other arithmetic  44.2 us (4%)
  local copies, waits for them, and re-layouts  41.9 us (4%)
  starting transfers between devices  21.3 us (2%)
  between operations  15 us (1%)
    ppermute x8, waiting for transfers between devices, swap_y(): return lax.ppermute(a, 'dp', [(i, i ^ 2) for i in range(4)])  314 us
    ppermute x9, waiting for transfers between devices, swap_row(): return lax.ppermute(a, 'row', [(0, 1), (1, 0)])  205 us
    all_gather x1, waiting for transfers between devices, local_units(): x0 = lax.all_gather(tokens, 'col', axis=1, tiled=True)  67.1 us
    dot_general x8, matrix products, contract_cols(): lax.dot_general(left, right, (((1,), (1,)), ((), ())), preferred_element_...  65.6 us
    all_gather x1, waiting for transfers between devices, local_units(): dy0 = lax.all_gather(cotangent, 'col', axis=1, tiled=True)  63.7 us
    dot_general x8, matrix products, contract_rows(): lax.dot_general(left, right, (((0,), (0,)), ((), ())), preferred_element_...  59.8 us
    pallas_call x4, Pallas kernels, place(): pl.pallas_call(functools.partial(place_body, parts, outs, 0 if previous i...  52.4 us
    dot_general x5, matrix products, forward(): mine = jnp.dot(a, w, preferred_element_type=f32).astype(bf16)  36.9 us
  transfers between devices with their start and end apart: 39, of which 13 were waited for; matrix products, arithmetic and copies ran while one was open for 25% of the time, Pallas kernels for 5%

profile of v1, /device:TPU:0, one launch (start us, length us, event | category | flops | bytes accessed | tf_op | source)
XLA Modules:
  0.0 1014.4 jit_solution(3868156339616485938)
XLA Ops:
  8.7 67.1 %all-gather.3.cloned.1.call-done = bf16[768,2048]{1,0:T(8,128)(2,1)} async-done(((bf16[768,512]{1,0:T(8,128)(2,1)}), bf16[768,2048]{1,0:T(8,128)(2,1)}) %all-gather.3.cloned.1.call-update) | async-done | bytes 3145744 | tf_op jit(solution)/shard_map/all_gather | solution.py:107
  75.8 63.7 %all-gather.5.cloned.1.call-done = bf16[768,2048]{1,0:T(8,128)(2,1)} async-done(((bf16[768,512]{1,0:T(8,128)(2,1)}), bf16[768,2048]{1,0:T(8,128)(2,1)}) %all-gather.5.cloned.1.call-update) | async-done | bytes 3145744 | tf_op jit(solution)/shard_map/all_gather | solution.py:110
  144.7 3.8 constant_dynamic-slice_fusion.2
  149.1 3.4 fusion.18
  156.4 7.2 fusion.19
  164.1 46.6 %collective-permute-done.15 = bf16[768,2048]{1,0:T(8,128)(2,1)S(1)} collective-permute-done((bf16[768,2048]{1,0:T(8,128)(2,1)}, bf16[768,2048]{1,0:T(8,128)(2,1)S(1)}, u32[]{:S(2)}, u32[]{:S(2)}) %collective-permute-start.15) | collective-permute-done | bytes 3145760 | tf_op jit(solution)/shard_map/ppermute | solution.py:98
  210.7 66.4 %collective-permute-done.5 = bf16[768,2048]{1,0:T(8,128)(2,1)} collective-permute-done((bf16[768,2048]{1,0:T(8,128)(2,1)}, bf16[768,2048]{1,0:T(8,128)(2,1)}, u32[]{:S(2)}, u32[]{:S(2)}) %collective-permute-start.5) | collective-permute-done | bytes 3145760 | tf_op jit(solution)/shard_map/ppermute | solution.py:98
  277.1 4.0 constant_dynamic-update-slice_fusion.3
  281.3 3.9 constant_dynamic-update-slice_fusion
  285.6 7.7 convolution_convert_fusion.6
  293.4 9.4 convolution_convert_fusion.4
  304.7 7.3 convolution_convert_fusion.3
  313.6 9.6 convolution_convert_fusion.2
  324.2 6.1 convolution_convert_fusion.7
  331.8 5.2 convolution_convert_fusion.5
  337.0 29.1 %collective-permute-done.8 = bf16[1536,768]{1,0:T(8,128)(2,1)S(1)} collective-permute-done((bf16[1536,768]{1,0:T(8,128)(2,1)S(1)}, bf16[1536,768]{1,0:T(8,128)(2,1)S(1)}, u32[]{:S(2)}, u32[]{:S(2)}) %collective-permute-start.8) | collective-permute-done | bytes 2359328 | tf_op jit(solution)/shard_map/ppermute | solution.py:92
  368.1 90.7 %collective-permute-done.18 = bf16[1536,384]{1,0:T(8,128)(2,1)S(1)} collective-permute-done((bf16[1536,384]{1,0:T(8,128)(2,1)S(1)}, bf16[1536,384]{1,0:T(8,128)(2,1)S(1)}, u32[]{:S(2)}, u32[]{:S(2)}) %collective-permute-start.18) | collective-permute-done | bytes 1179680 | tf_op jit(solution)/shard_map/ppermute | solution.py:92
  461.3 3.7 multiply_convert_fusion.7
  467.1 76.0 %collective-permute-done.17 = bf16[1536,512]{1,0:T(8,128)(2,1)} collective-permute-done((bf16[1536,512]{1,0:T(8,128)(2,1)S(1)}, bf16[1536,512]{1,0:T(8,128)(2,1)}, u32[]{:S(2)}, u32[]{:S(2)}) %collective-permute-start.17) | collective-permute-done | bytes 1572896 | tf_op jit(solution)/shard_map/ppermute | solution.py:92
  543.2 4.2 multiply_convert_fusion.1
  547.3 9.6 convolution_convert_fusion
  557.5 6.0 convolution_convert_fusion.8
  567.9 8.9 collective-permute-done.12
  576.8 3.8 multiply_convert_fusion.3
  580.6 8.2 fusion.15
  591.9 11.8 %add_convert_fusion = bf16[1536,2048]{1,0:T(8,128)(2,1)S(1)} fusion(f32[1536,2048]{1,0:T(8,128)} %fusion.15, bf16[1536,512]{1,0:T(8,128)(2,1)} %get-tuple-element.16, bf16[1536,512]{1,0:T(8,128)(2,1)} %get-tuple-element.15, bf16[2048,512]{1,0:T(8,128)(2,1)} %copy-done.17, bf16[2048,512]{1,0:T(8,128)(2,1)} %copy-done.20), kind=kOutput, calls=%fused_computation | convolution fusion | flops 6463422464 | bytes 26214400 | tf_op jit(solution)/shard_map/dot_general | solution.py:20
  605.1 11.7 %fusion.12 = f32[2048,1024]{1,0:T(8,128)} fusion(bf16[1536,2048]{1,0:T(8,128)(2,1)} %constant_dynamic-update-slice_fusion, bf16[1536,512]{1,0:T(8,128)(2,1)} %get-tuple-element.14, bf16[1536,512]{1,0:T(8,128)(2,1)S(1)} %copy-done.25), kind=kOutput, calls=%fused_computation.61 | convolution fusion | flops 6448742400 | bytes 17825792 | tf_op jit(solution)/shard_map/dot_general | solution.py:14
  616.8 5.0 fusion.39
  623.9 4.5 multiply_convert_fusion.9
  632.9 9.3 convolution_convert_fusion.1
  648.1 8.1 fusion.17
  656.3 12.4 %add_convert_fusion.1 = bf16[1536,2048]{1,0:T(8,128)(2,1)} fusion(f32[1536,2048]{1,0:T(8,128)} %fusion.17, bf16[1536,512]{1,0:T(8,128)(2,1)} %get-tuple-element.14, bf16[1536,512]{1,0:T(8,128)(2,1)S(1)} %copy-done.26, bf16[2048,512]{1,0:T(8,128)(2,1)S(1)} %copy-done.19, bf16[2048,512]{1,0:T(8,128)(2,1)S(1)} %copy-done.21), kind=kOutput, calls=%fused_computation.1 | convolution fusion | flops 6463422464 | bytes 26214400 | tf_op jit(solution)/shard_map/dot_general | solution.py:20
  668.7 4.1 slice.109
  675.6 7.2 fusion.16
  682.9 4.9 add_convert_fusion.7
  687.9 7.2 add_convert_fusion.9.refs_0_
  696.4 8.0 add_convert_fusion.8.refs_0_
  705.5 10.9 %add_convert_fusion.2.refs_0_.refs_1_ = bf16[2048,1024]{1,0:T(8,128)(2,1)} fusion(f32[2048,1024]{1,0:T(8,128)} %fusion.12, bf16[1536,2048]{1,0:T(8,128)(2,1)S(1)} %bitcast.40, bf16[1536,512]{1,0:T(8,128)(2,1)S(1)} %copy-done.23, bf16[1536,512]{1,0:T(8,128)(2,1)S(1)} %copy-done.22), kind=kOutput, calls=%fused_computation.2 | convolution fusion | flops 6452936704 | bytes 22020096 | tf_op jit(solution)/shard_map/dot_general | solution.py:14
  717.2 7.3 add_convert_fusion.3.refs_0_.refs_1_
  725.8 4.9 add_convert_fusion.5
  733.1 44.4 %collective-permute-done.31.refs_2_ = bf16[512,2048]{1,0:T(8,128)(2,1)} collective-permute-done((bf16[512,2048]{1,0:T(8,128)(2,1)}, bf16[512,2048]{1,0:T(8,128)(2,1)}, u32[]{:S(2)}, u32[]{:S(2)}) %collective-permute-start.31) | collective-permute-done | bytes 2097184 | tf_op jit(solution)/shard_map/ppermute | solution.py:98
  777.5 89.9 %collective-permute-done.25.refs_4_.refs_5_ = bf16[2048,1024]{1,0:T(8,128)(2,1)} collective-permute-done((bf16[2048,1024]{1,0:T(8,128)(2,1)}, bf16[2048,1024]{1,0:T(8,128)(2,1)}, u32[]{:S(2)}, u32[]{:S(2)}) %collective-permute-start.25) | collective-permute-done | bytes 4194336 | tf_op jit(solution)/shard_map/ppermute | solution.py:98
  869.2 65.2 %collective-permute-done.22.refs_4_.refs_5_ = bf16[2048,768]{1,0:T(8,128)(2,1)} collective-permute-done((bf16[2048,768]{1,0:T(8,128)(2,1)S(1)}, bf16[2048,768]{1,0:T(8,128)(2,1)}, u32[]{:S(2)}, u32[]{:S(2)}) %collective-permute-start.22) | collective-permute-done | bytes 3145760 | tf_op jit(solution)/shard_map/ppermute | solution.py:98
  936.0 7.2 collective-permute-done.32.refs_3_
  949.9 11.1 %shard_map.94.refs_4_ = bf16[3584,2048]{1,0:T(8,128)(2,1)} custom-call(s32[4]{0:T(128)S(1)} %pad_add_fusion.pos_ref, bf16[512,2048]{1,0:T(8,128)(2,1)} %add_convert_fusion.8.refs_0_, bf16[512,2048]{1,0:T(8,128)(2,1)S(1)} %copy-done.1, bf16[512,2048]{1,0:T(8,128)(2,1)} %collective-permute-done.31.refs_2_, bf16[512,2048]{1,0:T(8,128)(2,1)S(1)} %copy-done.3), custom_call_target="tpu_custom_call" | custom-call | bytes 16777216 | tf_op jit(solution)/shard_map/pallas_call | solution.py:68
  961.0 9.5 shard_map.95
  970.5 19.2 %shard_map.92 = (bf16[2048,3584]{1,0:T(8,128)(2,1)}, bf16[2048,3584]{1,0:T(8,128)(2,1)}) custom-call(s32[4]{0:T(128)S(1)} %pad_add_fusion.pos_ref, bf16[2048,1024]{1,0:T(8,128)(2,1)} %add_convert_fusion.2.refs_0_.refs_1_, bf16[2048,1024]{1,0:T(8,128)(2,1)} %add_convert_fusion.2.refs_0_.refs_1_, bf16[2048,1024]{1,0:T(8,128)(2,1)} %collective-permute-done.24.refs_2_.refs_3_, ...), custom_call_target="tpu_custom_call" | custom-call | bytes 33554432 | tf_op jit(solution)/shard_map/pallas_call | solution.py:68
  989.7 12.6 %shard_map.93 = (bf16[2048,3584]{1,0:T(8,128)(2,1)}, bf16[2048,3584]{1,0:T(8,128)(2,1)}) custom-call(s32[4]{0:T(128)S(1)} %pad_add_fusion.pos_ref, bf16[2048,768]{1,0:T(8,128)(2,1)S(1)} %add_convert_fusion.3.refs_0_.refs_1_, bf16[2048,768]{1,0:T(8,128)(2,1)S(1)} %add_convert_fusion.3.refs_0_.refs_1_, ...), custom_call_target="tpu_custom_call", output_to_operand_aliasing={{0}: (9, {}), {1}: (10, {})} | custom-call | bytes 25165824 | tf_op jit(solution)/shard_map/pallas_call | solution.py:68
  (214 shorter events, 71.6 us)
Async XLA Ops:
  7.2 68.6 %all-gather.3.cloned.1.call-start = ((), (), s32[]{:S(2)}) async-start(), calls=%async_computation.4 | async-start | bytes 3932160 | tf_op jit(solution)/shard_map/all_gather | solution.py:107
  7.9 131.6 %all-gather.5.cloned.1.call-start = ((), (), s32[]{:S(2)}) async-start(), calls=%async_computation.7 | async-start | bytes 3932160 | tf_op jit(solution)/shard_map/all_gather | solution.py:110
  8.7 935.9 %reduce-scatter.7.cloned.1.call-start = ((), (), s32[]{:S(2)}) async-start(), calls=%async_computation.6 | async-start | bytes 3932160 | tf_op jit(solution)/shard_map/reduce_scatter | solution.py:144
  75.8 80.6 %collective-permute-start = (bf16[768,2048]{1,0:T(8,128)(2,1)}, bf16[768,2048]{1,0:T(8,128)(2,1)}, u32[]{:S(2)}, u32[]{:S(2)}) collective-permute-start(bf16[768,2048]{1,0:T(8,128)(2,1)} %all-gather.3.cloned.1.call-done), channel_id=1, source_target_pairs={{0,8},{8,0},{16,24},{24,16},{1,9},{9,1},{17,25},{25,17},{2,10},{10... | collective-permute-start | bytes 9437192 | tf_op jit(solution)/shard_map/ppermute | solution.py:95
  139.5 71.2 %collective-permute-start.15 = (bf16[768,2048]{1,0:T(8,128)(2,1)}, bf16[768,2048]{1,0:T(8,128)(2,1)S(1)}, u32[]{:S(2)}, u32[]{:S(2)}) collective-permute-start(bf16[768,2048]{1,0:T(8,128)(2,1)} %all-gather.5.cloned.1.call-done), channel_id=1, source_target_pairs={{0,16},{8,24},{16,0},{24,8},{1,17},{9,25},{17,1},{25,9},{2,18},{10... | collective-permute-start | bytes 9437192 | tf_op jit(solution)/shard_map/ppermute | solution.py:98
  141.0 136.1 %collective-permute-start.5 = (bf16[768,2048]{1,0:T(8,128)(2,1)}, bf16[768,2048]{1,0:T(8,128)(2,1)}, u32[]{:S(2)}, u32[]{:S(2)}) collective-permute-start(bf16[768,2048]{1,0:T(8,128)(2,1)} %all-gather.3.cloned.1.call-done), channel_id=1, source_target_pairs={{0,16},{8,24},{16,0},{24,8},{1,17},{9,25},{17,1},{25,9},{2,18},{10... | collective-permute-start | bytes 9437192 | tf_op jit(solution)/shard_map/ppermute | solution.py:98
  144.7 140.5 %collective-permute-start.11 = (bf16[768,2048]{1,0:T(8,128)(2,1)S(1)}, bf16[768,2048]{1,0:T(8,128)(2,1)S(1)}, u32[]{:S(2)}, u32[]{:S(2)}) collective-permute-start(bf16[768,2048]{1,0:T(8,128)(2,1)S(1)} %copy-done.15), channel_id=1, source_target_pairs={{0,8},{8,0},{16,24},{24,16},{1,9},{9,1},{17,25},{25,17},{2,10},{10... | collective-permute-start | bytes 9437192 | tf_op jit(solution)/shard_map/ppermute | solution.py:95
  148.5 156.2 %copy-start.31 = (bf16[2048,384]{1,0:T(8,128)(2,1)}, bf16[2048,384]{1,0:T(8,128)(2,1)S(1)}, u32[]{:S(2)}) copy-start(bf16[2048,384]{1,0:T(8,128)(2,1)S(1)} %get-tuple-element.27) | copy-start | bytes 4718596
  148.5 156.1 %copy-start.34 = (bf16[2048,384]{1,0:T(8,128)(2,1)}, bf16[2048,384]{1,0:T(8,128)(2,1)S(1)}, u32[]{:S(2)}) copy-start(bf16[2048,384]{1,0:T(8,128)(2,1)S(1)} %get-tuple-element.28) | copy-start | bytes 4718596
  152.5 411.0 %collective-permute-start.1 = (bf16[768,1024]{1,0:T(8,128)(2,1)S(1)}, bf16[768,1024]{1,0:T(8,128)(2,1)}, u32[]{:S(2)}, u32[]{:S(2)}) collective-permute-start(bf16[768,1024]{1,0:T(8,128)(2,1)S(1)} %fusion.18), channel_id=1, source_target_pairs={{0,4},{4,0},{1,5},{5,1},{2,6},{6,2},{3,7},{7,3},{8,12},{12,8},{9,1... | collective-permute-start | bytes 4718600 | tf_op jit(solution)/shard_map/ppermute | solution.py:92
  163.6 401.4 %collective-permute-start.2 = (bf16[768,1024]{1,0:T(8,128)(2,1)}, bf16[768,1024]{1,0:T(8,128)(2,1)}, u32[]{:S(2)}, u32[]{:S(2)}) collective-permute-start(bf16[768,1024]{1,0:T(8,128)(2,1)} %fusion.19), channel_id=1, source_target_pairs={{0,4},{4,0},{1,5},{5,1},{2,6},{6,2},{3,7},{7,3},{8,12},{12,8},{9,1... | collective-permute-start | bytes 4718600 | tf_op jit(solution)/shard_map/ppermute | solution.py:92
  210.7 113.0 %collective-permute-start.16 = (bf16[768,2048]{1,0:T(8,128)(2,1)S(1)}, bf16[768,2048]{1,0:T(8,128)(2,1)S(1)}, u32[]{:S(2)}, u32[]{:S(2)}) collective-permute-start(bf16[768,2048]{1,0:T(8,128)(2,1)S(1)} %collective-permute-done.15), channel_id=1, source_target_pairs={{0,8},{8,0},{16,24},{24,16},{1,9},{9,1},{17,25},{25,17},{2,10},{10... | collective-permute-start | bytes 9437192 | tf_op jit(solution)/shard_map/ppermute | solution.py:95
  277.1 25.7 %collective-permute-start.6 = (bf16[768,2048]{1,0:T(8,128)(2,1)}, bf16[768,2048]{1,0:T(8,128)(2,1)S(1)}, u32[]{:S(2)}, u32[]{:S(2)}) collective-permute-start(bf16[768,2048]{1,0:T(8,128)(2,1)} %collective-permute-done.5), channel_id=1, source_target_pairs={{0,8},{8,0},{16,24},{24,16},{1,9},{9,1},{17,25},{25,17},{2,10},{10... | collective-permute-start | bytes 9437192 | tf_op jit(solution)/shard_map/ppermute | solution.py:95
  285.6 271.9 %copy-start.7 = (bf16[1536,2048]{1,0:T(8,128)(2,1)}, bf16[1536,2048]{1,0:T(8,128)(2,1)S(1)}, u32[]{:S(2)}) copy-start(bf16[1536,2048]{1,0:T(8,128)(2,1)S(1)} %constant_dynamic-update-slice_fusion.4) | copy-start | bytes 18874372
  312.0 54.1 %collective-permute-start.8 = (bf16[1536,768]{1,0:T(8,128)(2,1)S(1)}, bf16[1536,768]{1,0:T(8,128)(2,1)S(1)}, u32[]{:S(2)}, u32[]{:S(2)}) collective-permute-start(bf16[1536,768]{1,0:T(8,128)(2,1)S(1)} %convolution_convert_fusion.3), channel_id=1, source_target_pairs={{0,4},{4,0},{1,5},{5,1},{2,6},{6,2},{3,7},{7,3},{8,12},{12,8},{9,1... | collective-permute-start | bytes 7077896 | tf_op jit(solution)/shard_map/ppermute | solution.py:92
  323.1 141.9 %collective-permute-start.7 = (bf16[1536,1024]{1,0:T(8,128)(2,1)S(1)}, bf16[1536,1024]{1,0:T(8,128)(2,1)S(1)}, u32[]{:S(2)}, u32[]{:S(2)}) collective-permute-start(bf16[1536,1024]{1,0:T(8,128)(2,1)S(1)} %convolution_convert_fusion.2), channel_id=1, source_target_pairs={{0,4},{4,0},{1,5},{5,1},{2,6},{6,2},{3,7},{7,3},{8,12},{12,8},{9,1... | collective-permute-start | bytes 9437192 | tf_op jit(solution)/shard_map/ppermute | solution.py:92
  330.3 128.5 %collective-permute-start.18 = (bf16[1536,384]{1,0:T(8,128)(2,1)S(1)}, bf16[1536,384]{1,0:T(8,128)(2,1)S(1)}, u32[]{:S(2)}, u32[]{:S(2)}) collective-permute-start(bf16[1536,384]{1,0:T(8,128)(2,1)S(1)} %convolution_convert_fusion.7), channel_id=1, source_target_pairs={{0,4},{4,0},{1,5},{5,1},{2,6},{6,2},{3,7},{7,3},{8,12},{12,8},{9,1... | collective-permute-start | bytes 3538952 | tf_op jit(solution)/shard_map/ppermute | solution.py:92
  337.0 121.8 %copy-start.29 = (bf16[1536,512]{1,0:T(8,128)(2,1)}, bf16[1536,512]{1,0:T(8,128)(2,1)S(1)}, u32[]{:S(2)}) copy-start(bf16[1536,512]{1,0:T(8,128)(2,1)S(1)} %convolution_convert_fusion.5) | copy-start | bytes 4718596
  366.1 255.7 %collective-permute-start.3 = (bf16[1536,768]{1,0:T(8,128)(2,1)}, bf16[1536,768]{1,0:T(8,128)(2,1)S(1)}, u32[]{:S(2)}, u32[]{:S(2)}) collective-permute-start(bf16[1536,768]{1,0:T(8,128)(2,1)} %convolution_convert_fusion.4), channel_id=1, source_target_pairs={{0,4},{4,0},{1,5},{5,1},{2,6},{6,2},{3,7},{7,3},{8,12},{12,8},{9,1... | collective-permute-start | bytes 7077896 | tf_op jit(solution)/shard_map/ppermute | solution.py:92
  368.1 96.9 %copy-start.24 = (bf16[1536,512]{1,0:T(8,128)(2,1)S(1)}, bf16[1536,512]{1,0:T(8,128)(2,1)}, u32[]{:S(2)}) copy-start(bf16[1536,512]{1,0:T(8,128)(2,1)} %convolution_convert_fusion.6) | copy-start | bytes 4718596
  459.8 83.3 %collective-permute-start.17 = (bf16[1536,512]{1,0:T(8,128)(2,1)S(1)}, bf16[1536,512]{1,0:T(8,128)(2,1)}, u32[]{:S(2)}, u32[]{:S(2)}) collective-permute-start(bf16[1536,512]{1,0:T(8,128)(2,1)S(1)} %convolution_convert_fusion.5), channel_id=1, source_target_pairs={{0,4},{4,0},{1,5},{5,1},{2,6},{6,2},{3,7},{7,3},{8,12},{12,8},{9,1... | collective-permute-start | bytes 4718600 | tf_op jit(solution)/shard_map/ppermute | solution.py:92
  465.0 82.3 %copy-start.12 = (bf16[1536,384]{1,0:T(8,128)(2,1)}, bf16[1536,384]{1,0:T(8,128)(2,1)S(1)}, u32[]{:S(2)}) copy-start(bf16[1536,384]{1,0:T(8,128)(2,1)S(1)} %get-tuple-element.24) | copy-start | bytes 3538948
  465.0 115.5 %copy-start.37 = (bf16[1536,384]{1,0:T(8,128)(2,1)}, bf16[1536,384]{1,0:T(8,128)(2,1)S(1)}, u32[]{:S(2)}) copy-start(bf16[1536,384]{1,0:T(8,128)(2,1)S(1)} %get-tuple-element.19) | copy-start | bytes 3538948
  465.0 78.1 %copy-start.30 = (bf16[1536,512]{1,0:T(8,128)(2,1)S(1)}, bf16[1536,512]{1,0:T(8,128)(2,1)}, u32[]{:S(2)}) copy-start(bf16[1536,512]{1,0:T(8,128)(2,1)} %copy-done.29) | copy-start | bytes 4718596
  465.1 111.7 %collective-permute-start.12 = (bf16[1536,512]{1,0:T(8,128)(2,1)S(1)}, bf16[1536,512]{1,0:T(8,128)(2,1)S(1)}, u32[]{:S(2)}, u32[]{:S(2)}) collective-permute-start(bf16[1536,512]{1,0:T(8,128)(2,1)S(1)} %copy-done.24), channel_id=1, source_target_pairs={{0,4},{4,0},{1,5},{5,1},{2,6},{6,2},{3,7},{7,3},{8,12},{12,8},{9,1... | collective-permute-start | bytes 4718600 | tf_op jit(solution)/shard_map/ppermute | solution.py:92
  557.4 31.3 %collective-permute-start.9 = (bf16[768,2048]{1,0:T(8,128)(2,1)S(1)}, bf16[768,2048]{1,0:T(8,128)(2,1)S(1)}, u32[]{:S(2)}, u32[]{:S(2)}) collective-permute-start(bf16[768,2048]{1,0:T(8,128)(2,1)S(1)} %slice.107), channel_id=1, source_target_pairs={{0,8},{8,0},{16,24},{24,16},{1,9},{9,1},{17,25},{25,17},{2,10},{10... | collective-permute-start | bytes 9437192 | tf_op jit(solution)/shard_map/ppermute | solution.py:95
  563.5 60.4 %collective-permute-start.13 = (bf16[1536,384]{1,0:T(8,128)(2,1)}, bf16[1536,384]{1,0:T(8,128)(2,1)}, u32[]{:S(2)}, u32[]{:S(2)}) collective-permute-start(bf16[1536,384]{1,0:T(8,128)(2,1)} %convolution_convert_fusion.8), channel_id=1, source_target_pairs={{0,4},{4,0},{1,5},{5,1},{2,6},{6,2},{3,7},{7,3},{8,12},{12,8},{9,1... | collective-permute-start | bytes 3538952 | tf_op jit(solution)/shard_map/ppermute | solution.py:92
  591.8 353.9 %reduce-scatter.11.cloned.1.call-start = ((), (), s32[]{:S(2)}) async-start(), calls=%async_computation.9 | async-start | bytes 3932160 | tf_op jit(solution)/shard_map/reduce_scatter | solution.py:144
  604.1 24.4 %collective-permute-start.19 = (bf16[768,2048]{1,0:T(8,128)(2,1)S(1)}, bf16[768,2048]{1,0:T(8,128)(2,1)S(1)}, u32[]{:S(2)}, u32[]{:S(2)}) collective-permute-start(bf16[768,2048]{1,0:T(8,128)(2,1)S(1)} %slice.111), channel_id=1, source_target_pairs={{0,8},{8,0},{16,24},{24,16},{1,9},{9,1},{17,25},{25,17},{2,10},{10... | collective-permute-start | bytes 9437192 | tf_op jit(solution)/shard_map/ppermute | solution.py:95
  631.5 370.7 %reduce-scatter.5.cloned.1.call-start = ((), (), s32[]{:S(2)}) async-start(), calls=%async_computation.5 | async-start | bytes 3932160 | tf_op jit(solution)/shard_map/reduce_scatter | solution.py:145
  646.9 35.9 %collective-permute-start.4 = (bf16[768,2048]{1,0:T(8,128)(2,1)}, bf16[768,2048]{1,0:T(8,128)(2,1)}, u32[]{:S(2)}, u32[]{:S(2)}) collective-permute-start(bf16[768,2048]{1,0:T(8,128)(2,1)} %slice.101), channel_id=1, source_target_pairs={{0,8},{8,0},{16,24},{24,16},{1,9},{9,1},{17,25},{25,17},{2,10},{10... | collective-permute-start | bytes 9437192 | tf_op jit(solution)/shard_map/ppermute | solution.py:95
  672.8 51.7 %collective-permute-start.14 = (bf16[768,2048]{1,0:T(8,128)(2,1)}, bf16[768,2048]{1,0:T(8,128)(2,1)}, u32[]{:S(2)}, u32[]{:S(2)}) collective-permute-start(bf16[768,2048]{1,0:T(8,128)(2,1)} %slice.109), channel_id=1, source_target_pairs={{0,8},{8,0},{16,24},{24,16},{1,9},{9,1},{17,25},{25,17},{2,10},{10... | collective-permute-start | bytes 9437192 | tf_op jit(solution)/shard_map/ppermute | solution.py:95
  687.8 317.0 %reduce-scatter.9.cloned.1.call-start = ((), (), s32[]{:S(2)}) async-start(), calls=%async_computation.8 | async-start | bytes 3932160 | tf_op jit(solution)/shard_map/reduce_scatter | solution.py:145
  695.1 37.5 %collective-permute-start.28 = (bf16[384,2048]{1,0:T(8,128)(2,1)}, bf16[384,2048]{1,0:T(8,128)(2,1)}, u32[]{:S(2)}, u32[]{:S(2)}) collective-permute-start(bf16[384,2048]{1,0:T(8,128)(2,1)} %add_convert_fusion.9.refs_0_), channel_id=1, source_target_pairs={{0,16},{8,24},{16,0},{24,8},{1,17},{9,25},{17,1},{25,9},{2,18},{10... | collective-permute-start | bytes 4718600 | tf_op jit(solution)/shard_map/ppermute | solution.py:98
  696.1 36.4 %collective-permute-start.27 = (bf16[384,2048]{1,0:T(8,128)(2,1)}, bf16[384,2048]{1,0:T(8,128)(2,1)}, u32[]{:S(2)}, u32[]{:S(2)}) collective-permute-start(bf16[384,2048]{1,0:T(8,128)(2,1)} %add_convert_fusion.9.refs_0_), channel_id=1, source_target_pairs={{0,8},{8,0},{16,24},{24,16},{1,9},{9,1},{17,25},{25,17},{2,10},{10... | collective-permute-start | bytes 4718600 | tf_op jit(solution)/shard_map/ppermute | solution.py:95
  696.4 29.4 %slice-start.4 = ((s8[6291456]{0:T(1024)(128)(4,1)}), s8[4194304]{0:T(1024)(128)(4,1)S(1)}, s32[]{:S(2)}) async-start(s8[6291456]{0:T(1024)(128)(4,1)} %bitcast.33), calls=%async_computation.14 | async-start | bytes 8388608
  704.4 73.1 %collective-permute-start.31 = (bf16[512,2048]{1,0:T(8,128)(2,1)}, bf16[512,2048]{1,0:T(8,128)(2,1)}, u32[]{:S(2)}, u32[]{:S(2)}) collective-permute-start(bf16[512,2048]{1,0:T(8,128)(2,1)} %add_convert_fusion.8.refs_0_), channel_id=1, source_target_pairs={{0,16},{8,24},{16,0},{24,8},{1,17},{9,25},{17,1},{25,9},{2,18},{10... | collective-permute-start | bytes 6291464 | tf_op jit(solution)/shard_map/ppermute | solution.py:98
  716.4 151.0 %collective-permute-start.25 = (bf16[2048,1024]{1,0:T(8,128)(2,1)}, bf16[2048,1024]{1,0:T(8,128)(2,1)}, u32[]{:S(2)}, u32[]{:S(2)}) collective-permute-start(bf16[2048,1024]{1,0:T(8,128)(2,1)} %add_convert_fusion.2.refs_0_.refs_1_), channel_id=1, source_target_pairs={{0,16},{8,24},{16,0},{24,8},{1,17},{9,25},{17,1},{25,9},{2,18},{10... | collective-permute-start | bytes 12582920 | tf_op jit(solution)/shard_map/ppermute | solution.py:98
  724.5 209.8 %collective-permute-start.22 = (bf16[2048,768]{1,0:T(8,128)(2,1)S(1)}, bf16[2048,768]{1,0:T(8,128)(2,1)}, u32[]{:S(2)}, u32[]{:S(2)}) collective-permute-start(bf16[2048,768]{1,0:T(8,128)(2,1)S(1)} %add_convert_fusion.3.refs_0_.refs_1_), channel_id=1, source_target_pairs={{0,16},{8,24},{16,0},{24,8},{1,17},{9,25},{17,1},{25,9},{2,18},{10... | collective-permute-start | bytes 9437192 | tf_op jit(solution)/shard_map/ppermute | solution.py:98
  732.6 134.8 %collective-permute-start.30 = (bf16[512,2048]{1,0:T(8,128)(2,1)}, bf16[512,2048]{1,0:T(8,128)(2,1)S(1)}, u32[]{:S(2)}, u32[]{:S(2)}) collective-permute-start(bf16[512,2048]{1,0:T(8,128)(2,1)} %add_convert_fusion.8.refs_0_), channel_id=1, source_target_pairs={{0,8},{8,0},{16,24},{24,16},{1,9},{9,1},{17,25},{25,17},{2,10},{10... | collective-permute-start | bytes 6291464 | tf_op jit(solution)/shard_map/ppermute | solution.py:95
  732.6 213.1 %collective-permute-start.24 = (bf16[2048,1024]{1,0:T(8,128)(2,1)}, bf16[2048,1024]{1,0:T(8,128)(2,1)}, u32[]{:S(2)}, u32[]{:S(2)}) collective-permute-start(bf16[2048,1024]{1,0:T(8,128)(2,1)} %add_convert_fusion.2.refs_0_.refs_1_), channel_id=1, source_target_pairs={{0,8},{8,0},{16,24},{24,16},{1,9},{9,1},{17,25},{25,17},{2,10},{10... | collective-permute-start | bytes 12582920 | tf_op jit(solution)/shard_map/ppermute | solution.py:95
  777.5 156.9 %collective-permute-start.29 = (bf16[384,2048]{1,0:T(8,128)(2,1)}, bf16[384,2048]{1,0:T(8,128)(2,1)S(1)}, u32[]{:S(2)}, u32[]{:S(2)}) collective-permute-start(bf16[384,2048]{1,0:T(8,128)(2,1)} %collective-permute-done.28.refs_2_), channel_id=1, source_target_pairs={{0,8},{8,0},{16,24},{24,16},{1,9},{9,1},{17,25},{25,17},{2,10},{10... | collective-permute-start | bytes 4718600 | tf_op jit(solution)/shard_map/ppermute | solution.py:95
  867.4 103.1 %collective-permute-start.26 = (bf16[2048,1024]{1,0:T(8,128)(2,1)}, bf16[2048,1024]{1,0:T(8,128)(2,1)}, u32[]{:S(2)}, u32[]{:S(2)}) collective-permute-start(bf16[2048,1024]{1,0:T(8,128)(2,1)} %collective-permute-done.25.refs_4_.refs_5_), channel_id=1, source_target_pairs={{0,8},{8,0},{16,24},{24,16},{1,9},{9,1},{17,25},{25,17},{2,10},{10... | collective-permute-start | bytes 12582920 | tf_op jit(solution)/shard_map/ppermute | solution.py:95
  868.7 120.9 %collective-permute-start.21 = (bf16[2048,768]{1,0:T(8,128)(2,1)S(1)}, bf16[2048,768]{1,0:T(8,128)(2,1)}, u32[]{:S(2)}, u32[]{:S(2)}) collective-permute-start(bf16[2048,768]{1,0:T(8,128)(2,1)S(1)} %add_convert_fusion.3.refs_0_.refs_1_), channel_id=1, source_target_pairs={{0,8},{8,0},{16,24},{24,16},{1,9},{9,1},{17,25},{25,17},{2,10},{10... | collective-permute-start | bytes 9437192 | tf_op jit(solution)/shard_map/ppermute | solution.py:95
  934.4 55.3 %collective-permute-start.23 = (bf16[2048,768]{1,0:T(8,128)(2,1)}, bf16[2048,768]{1,0:T(8,128)(2,1)}, u32[]{:S(2)}, u32[]{:S(2)}) collective-permute-start(bf16[2048,768]{1,0:T(8,128)(2,1)} %collective-permute-done.22.refs_4_.refs_5_), channel_id=1, source_target_pairs={{0,8},{8,0},{16,24},{24,16},{1,9},{9,1},{17,25},{25,17},{2,10},{10... | collective-permute-start | bytes 9437192 | tf_op jit(solution)/shard_map/ppermute | solution.py:95
  935.5 7.7 collective-permute-start.32
  944.6 57.7 %collective-permute-start.10 = (bf16[192,2048]{1,0:T(8,128)(2,1)}, bf16[192,2048]{1,0:T(8,128)(2,1)}, u32[]{:S(2)}, u32[]{:S(2)}) collective-permute-start(bf16[192,2048]{1,0:T(8,128)(2,1)} %reduce-scatter.7.cloned.1.call-done), channel_id=1, source_target_pairs={{0,16},{8,24},{16,0},{24,8},{1,17},{9,25},{17,1},{25,9},{2,18},{10... | collective-permute-start | bytes 2359304 | tf_op jit(solution)/shard_map/ppermute | solution.py:98
  945.7 59.1 %collective-permute-start.20 = (bf16[192,2048]{1,0:T(8,128)(2,1)}, bf16[192,2048]{1,0:T(8,128)(2,1)}, u32[]{:S(2)}, u32[]{:S(2)}) collective-permute-start(bf16[192,2048]{1,0:T(8,128)(2,1)} %reduce-scatter.11.cloned.1.call-done), channel_id=1, source_target_pairs={{0,16},{8,24},{16,0},{24,8},{1,17},{9,25},{17,1},{25,9},{2,18},{10... | collective-permute-start | bytes 2359304 | tf_op jit(solution)/shard_map/ppermute | solution.py:98
  (49 other events, 397.2 us)
Sparse Core Ops, SparseCore 0:
  9.6 66.1 all-gather.2
  77.3 62.1 all-gather.4
  592.0 59.0 reduce-scatter.6
  653.2 60.2 reduce-scatter.10
  715.7 60.2 reduce-scatter.4
  778.1 60.2 reduce-scatter.8

commit v2 on v1

--- a/solution.py
+++ b/solution.py
@@ -104,93 +104,148 @@
     gu_w = [jnp.concatenate([gate_w[:, o : o + w], up_w[:, o : o + w]], axis=1) for o, w in bands]
     d_w = [down_w[o : o + w] for o, w in bands]
 
-    x0 = lax.all_gather(tokens, "col", axis=1, tiled=True)
-    x2 = swap_y(x0)
-    x1, x3 = swap_core(x0), swap_core(x2)
-    dy0 = lax.all_gather(cotangent, "col", axis=1, tiled=True)
-    dy2 = swap_y(dy0)
-    dy1, dy3 = swap_core(dy0), swap_core(dy2)
-    x = [jnp.concatenate([x0, x1], axis=0), jnp.concatenate([x2, x3], axis=0)]
-    dy = [jnp.concatenate([dy0, dy1], axis=0), jnp.concatenate([dy2, dy3], axis=0)]
+    def after(done, *values):
+        tied = lax.optimization_barrier((values, done))[0]
+        return tied if len(values) > 1 else tied[0]
+
+    def halves(near, far):
+        return jnp.concatenate([near, far], axis=0)
 
     def forward(a, w):
-        mine = jnp.dot(a, w, preferred_element_type=f32).astype(bf16)
-        return mine, swap_row(mine)
-
-    gu = [[None, None], [None, None]]
-    early = [forward(x0, gu_w[0]), forward(x1, gu_w[0])]
-    gu[0][0] = tuple(jnp.concatenate([early[0][i], early[1][i]], axis=0) for i in range(2))
-    gu[0][1] = forward(x[1], gu_w[0])
-    gu[1][0] = forward(x[0], gu_w[1])
-    gu[1][1] = forward(x[1], gu_w[1])
-
-    def gates(band, half):
-        mine, theirs = gu[band][half]
+        return jnp.dot(a, w, preferred_element_type=f32).astype(bf16)
+
+    def gates(band, mine, theirs):
         both = mine.astype(f32) + theirs.astype(f32)
         w = bands[band][1]
         gate, up = both[:, :w], both[:, w:]
         return gate, up, jax.nn.sigmoid(gate)
 
-    hidden = [[None, None], [None, None]]
-    for band in range(2):
-        for half in range(2):
-            gate, up, sigma = gates(band, half)
-            hidden[band][half] = (gate * sigma * up).astype(bf16)
-
-    def reduce_groups(halves):
-        sums = [
-            (a[:rows].astype(f32) + swap_core(a[rows:]).astype(f32)).astype(bf16) for a in halves
-        ]
-        far = lax.psum_scatter(sums[1], "col", scatter_dimension=0, tiled=True)
-        near = lax.psum_scatter(sums[0], "col", scatter_dimension=0, tiled=True)
-        return (near.astype(f32) + swap_y(far).astype(f32)).astype(bf16)
-
-    layer_out = reduce_groups(
-        [
-            jnp.dot(
-                jnp.concatenate([hidden[0][half], hidden[1][half]], axis=1),
-                down_w,
-                preferred_element_type=f32,
-            ).astype(bf16)
-            for half in range(2)
-        ]
-    )
-
-    def spread(a):
-        far = swap_y(a)
+    def activate(band, gu):
+        gate, up, sigma = gates(band, *gu)
+        return (gate * sigma * up).astype(bf16)
+
+    def backward(band, gu, mine, theirs):
+        gate, up, sigma = gates(band, *gu)
+        hidden_grad = mine.astype(f32) + theirs.astype(f32)
+        gate_grad = hidden_grad * up * sigma * (1.0 + gate * (1.0 - sigma))
+        up_grad = hidden_grad * (gate * sigma)
+        return jnp.concatenate([gate_grad.astype(bf16), up_grad.astype(bf16)], axis=1)
+
+    def core_sum(a):
+        return (a[:rows].astype(f32) + swap_core(a[rows:]).astype(f32)).astype(bf16)
+
+    def scatter(a):
+        return lax.psum_scatter(a, "col", scatter_dimension=0, tiled=True)
+
+    def spread(a, far):
         return [a, swap_core(a), far, swap_core(far)]
 
     pos = jnp.stack([me, me ^ 1, me ^ 2, me ^ 3]).astype(jnp.int32)
-    down_wgrad, gu_wgrad = None, None
-    for band in range(2):
-        o, w = bands[band]
-        part = contract_rows(hidden[band][0], dy[0]) + contract_rows(hidden[band][1], dy[1])
-        down_wgrad = place(pos, spread(part.astype(bf16)), down_wgrad, total, o, w, 1, 0)
-
-    grads = [[None, None], [None, None]]
-    for band in range(2):
-        o, w = bands[band]
-        for half in (1, 0):
-            mine = contract_cols(dy[half], d_w[band]).astype(bf16)
-            hidden_grad = mine.astype(f32) + swap_row(mine).astype(f32)
-            gate, up, sigma = gates(band, half)
-            gate_grad = hidden_grad * up * sigma * (1.0 + gate * (1.0 - sigma))
-            up_grad = hidden_grad * (gate * sigma)
-            grads[band][half] = jnp.concatenate(
-                [gate_grad.astype(bf16), up_grad.astype(bf16)], axis=1
-            )
-        part = contract_rows(x[0], grads[band][0]) + contract_rows(x[1], grads[band][1])
-        gu_wgrad = place(pos, spread(part.astype(bf16)), gu_wgrad, total, o, w, 2, 1)
-
-    input_grad = reduce_groups(
-        [
-            (
-                contract_cols(grads[0][half], gu_w[0]) + contract_cols(grads[1][half], gu_w[1])
-            ).astype(bf16)
-            for half in range(2)
-        ]
-    )
-    return layer_out, input_grad, gu_wgrad[0], gu_wgrad[1], down_wgrad[0]
+
+    x0 = lax.all_gather(tokens, "col", axis=1, tiled=True)
+    dy0 = lax.all_gather(after(x0, cotangent), "col", axis=1, tiled=True)
+    x2 = swap_y(x0)
+    x1 = swap_core(x0)
+
+    a0 = forward(x0, gu_w[0])
+    a0_in = swap_row(a0)
+    a1 = forward(after(a0, x1), gu_w[0])
+    a1_in = swap_row(a1)
+    x_near = halves(x0, x1)
+    b_near = forward(after(a1, x_near), gu_w[1])
+    b_near_in = swap_row(b_near)
+    ha0 = activate(0, after(b_near, a0, a0_in))
+    dy0 = after(ha0, dy0)
+    dy2 = swap_y(dy0)
+    dy1 = swap_core(dy0)
+
+    x3 = swap_core(x2)
+    x_far = halves(x2, x3)
+    a_far = forward(after(ha0, x_far), gu_w[0])
+    a_far_in = swap_row(a_far)
+    ha1 = activate(0, after(a_far, a1, a1_in))
+    b_far = forward(after(ha1, x_far), gu_w[1])
+    b_far_in = swap_row(b_far)
+    dy_near = halves(dy0, dy1)
+    ga_near = contract_cols(after(b_far, dy_near), d_w[0]).astype(bf16)
+    ga_near_in = swap_row(ga_near)
+    hb_near = activate(1, after(ga_near, b_near, b_near_in))
+    ha_near = halves(ha0, ha1)
+    h_near = jnp.concatenate([ha_near, hb_near], axis=1)
+    out_near = forward(h_near, down_w)
+    dy3 = swap_core(dy2)
+    dy_far = halves(dy2, dy3)
+    ga_far = contract_cols(after(out_near, dy_far), d_w[0]).astype(bf16)
+    ga_far_in = swap_row(ga_far)
+    near_sum = core_sum(after(ga_far, out_near))
+    near = scatter(near_sum)
+
+    ha_far = activate(0, after(ga_far, a_far, a_far_in))
+    down_a = (contract_rows(ha_near, dy_near) + contract_rows(ha_far, dy_far)).astype(bf16)
+    down_a_in = swap_y(down_a)
+    gb_far = contract_cols(after((down_a, near_sum), dy_far), d_w[1]).astype(bf16)
+    gb_far_in = swap_row(gb_far)
+    gb_near = contract_cols(after(gb_far, dy_near), d_w[1]).astype(bf16)
+    gb_near_in = swap_row(gb_near)
+    hb_far = activate(1, after(gb_near, b_far, b_far_in))
+    h_tied = after((hb_far, ga_near_in, near), hb_near, hb_far)
+    down_b = (contract_rows(h_tied[0], dy_near) + contract_rows(h_tied[1], dy_far)).astype(bf16)
+    out_far = forward(
+        after((down_b, down_a_in, ga_far_in), jnp.concatenate([ha_far, hb_far], axis=1)), down_w
+    )
+    far_sum = core_sum(out_far)
+    far = scatter(far_sum)
+    down_b_in = swap_y(down_b)
+    down_wgrad = place(
+        pos, list(after(out_far, *spread(down_a, down_a_in))), None, total, *bands[0], 1, 0
+    )
+
+    ga_tied = after((far_sum, down_wgrad, ga_far_in), a0, a0_in, a1, a1_in, ga_near, ga_near_in)
+    qa_near = backward(
+        0, (halves(ga_tied[0], ga_tied[2]), halves(ga_tied[1], ga_tied[3])), *ga_tied[4:]
+    )
+    ga_tied = after((qa_near, down_b_in), a_far, a_far_in, ga_far, ga_far_in)
+    qa_far = backward(0, ga_tied[:2], *ga_tied[2:])
+
+    def weight_part(near, far):
+        return (contract_rows(x_near, near) + contract_rows(x_far, far)).astype(bf16)
+
+    wa, wb = bands[0][1], bands[1][1]
+    gate_a = weight_part(qa_near[:, :wa], qa_far[:, :wa])
+    gate_a_in = swap_y(gate_a)
+    gb_tied = after((gate_a, gb_near_in), b_far, b_far_in, gb_far, gb_far_in)
+    qb_far = backward(1, gb_tied[:2], *gb_tied[2:])
+    ig_far = (contract_cols(qa_far, gu_w[0]) + contract_cols(qb_far, gu_w[1])).astype(bf16)
+    ig_far_sum = core_sum(ig_far)
+    ig_far_out = scatter(ig_far_sum)
+    q_tied = after((ig_far, gb_near_in, gate_a_in, far), qa_near, qa_far)
+    up_a = weight_part(q_tied[0][:, wa:], q_tied[1][:, wa:])
+    up_a_in = swap_y(up_a)
+    gb_tied = after((up_a, ig_far_sum), b_near, b_near_in, gb_near, gb_near_in)
+    qb_near = backward(1, gb_tied[:2], *gb_tied[2:])
+    q_tied = (qa_near, qb_near)
+    ig_near = (contract_cols(q_tied[0], gu_w[0]) + contract_cols(q_tied[1], gu_w[1])).astype(bf16)
+    ig_near_sum = core_sum(ig_near)
+    ig_near_out = scatter(ig_near_sum)
+    q_tied = after(ig_near, qb_near, qb_far)
+    gate_b = weight_part(q_tied[0][:, :wb], q_tied[1][:, :wb])
+    gate_b_in = swap_y(gate_b)
+    q_tied = after((gate_b, ig_near_sum), qb_near, qb_far)
+    up_b = weight_part(q_tied[0][:, wb:], q_tied[1][:, wb:])
+    up_b_in = swap_y(up_b)
+
+    down_pieces = list(after(up_b, *spread(down_b, down_b_in)))
+    down_wgrad = place(pos, down_pieces, down_wgrad, total, *bands[1], 1, 0)
+    gate_pieces = list(after(down_wgrad, *spread(gate_a, gate_a_in)))
+    gate_wgrad = place(pos, gate_pieces, None, total, *bands[0], 1, 1)
+    layer_out = (near.astype(f32) + swap_y(after(gate_wgrad, far)).astype(f32)).astype(bf16)
+    up_pieces = list(after((gate_wgrad, ig_far_out), *spread(up_a, up_a_in)))
+    up_wgrad = place(pos, up_pieces, None, total, *bands[0], 1, 1)
+    gate_pieces = list(after(up_wgrad, *spread(gate_b, gate_b_in)))
+    gate_wgrad = place(pos, gate_pieces, gate_wgrad, total, *bands[1], 1, 1)
+    up_wgrad = place(pos, spread(up_b, up_b_in), up_wgrad, total, *bands[1], 1, 1)
+    input_grad = (ig_near_out.astype(f32) + swap_y(ig_far_out).astype(f32)).astype(bf16)
+    return layer_out, input_grad, gate_wgrad[0], up_wgrad[0], down_wgrad[0]
 
 
 def local(tokens, cotangent, gate_weight, up_weight, down_weight):

time: 1020 us -> 845 us (0.83)
  waiting for transfers between devices: 658 us -> 431 us
  other arithmetic: 44.2 us -> 70.3 us
  Pallas kernels: 52.4 us -> 69 us
    ppermute x8 -> x10, waiting for transfers between devices: 314 us -> 208 us  [swap_y(): return lax.ppermute(a, 'dp', [(i, i ^ 2) for i in range(4)])]
    ppermute x9, waiting for transfers between devices: 205 us -> 132 us  [swap_row(): return lax.ppermute(a, 'row', [(0, 1), (1, 0)])]
    all_gather x1, waiting for transfers between devices: 63.7 us -> 0.01 us  [local_units(): dy0 = lax.all_gather(after(x0, cotangent), 'col', axis=1, tiled=True)]
    add x4 -> x9, other arithmetic: 6.99 us -> 24.8 us  [gates(): both = mine.astype(f32) + theirs.astype(f32)]
    pallas_call x4 -> x6, Pallas kernels: 52.4 us -> 69 us  [place(): pl.pallas_call(functools.partial(place_body, parts, outs, 0 if previous i...]
    ppermute x16 -> x20, waiting for transfers between devices: 7.25 us -> 21.9 us  [swap_core(): return lax.ppermute(a, 'dp', [(i, i ^ 1) for i in range(4)])]
    dot_general x8 -> x12, matrix products: 59.8 us -> 68.8 us  [contract_rows(): lax.dot_general(left, right, (((0,), (0,)), ((), ())), preferred_element_...]
    unnamed x120 -> x124, local copies, waits for them, and re-layouts: 22.1 us -> 19.5 us
  transfers between devices with their start and end apart: 39 -> 45, of which waited for: 13 -> 16; matrix products, arithmetic and copies ran while one was open for 25% -> 31% of each run, Pallas kernels for 5% -> 8%
where the time goes in v2:
time: 845 us; the launch traced here: 839 us
  waiting for transfers between devices  431 us (51%)
  matrix products  190 us (22%)
  other arithmetic  70.3 us (8%)
  Pallas kernels  69 us (8%)
  local copies, waits for them, and re-layouts  36.4 us (4%)
  starting transfers between devices  27.8 us (3%)
  between operations  15.4 us (2%)
    ppermute x10, waiting for transfers between devices, swap_y(): return lax.ppermute(a, 'dp', [(i, i ^ 2) for i in range(4)])  208 us
    ppermute x9, waiting for transfers between devices, swap_row(): return lax.ppermute(a, 'row', [(0, 1), (1, 0)])  132 us
    pallas_call x6, Pallas kernels, place(): pl.pallas_call(functools.partial(place_body, parts, outs, 0 if previous i...  69 us
    dot_general x12, matrix products, contract_rows(): lax.dot_general(left, right, (((0,), (0,)), ((), ())), preferred_element_...  68.8 us
    all_gather x1, waiting for transfers between devices, local_units(): x0 = lax.all_gather(tokens, 'col', axis=1, tiled=True)  67.8 us
    dot_general x8, matrix products, contract_cols(): lax.dot_general(left, right, (((1,), (1,)), ((), ())), preferred_element_...  63.5 us
    dot_general x7, matrix products, forward(): return jnp.dot(a, w, preferred_element_type=f32).astype(bf16)  57.3 us
    add x9, other arithmetic, gates(): both = mine.astype(f32) + theirs.astype(f32)  24.8 us
  transfers between devices with their start and end apart: 45, of which 16 were waited for; matrix products, arithmetic and copies ran while one was open for 31% of the time, Pallas kernels for 8%

profile of v2, /device:TPU:0, one launch (start us, length us, event | category | flops | bytes accessed | tf_op | source)
XLA Modules:
  0.0 839.2 jit_solution(5906301902813261614)
XLA Ops:
  7.9 67.8 %all-gather.3.cloned.1.call-done = bf16[768,2048]{1,0:T(8,128)(2,1)} async-done(((bf16[768,512]{1,0:T(8,128)(2,1)}), bf16[768,2048]{1,0:T(8,128)(2,1)}) %all-gather.3.cloned.1.call-update) | async-done | bytes 3145744 | tf_op jit(solution)/shard_map/all_gather | solution.py:145
  81.1 4.5 constant_dynamic-slice_fusion
  85.7 6.8 fusion.33
  95.2 6.9 convolution_convert_fusion.9
  103.6 42.9 %collective-permute-done.3 = bf16[768,2048]{1,0:T(8,128)(2,1)S(1)} collective-permute-done((bf16[768,2048]{1,0:T(8,128)(2,1)}, bf16[768,2048]{1,0:T(8,128)(2,1)S(1)}, u32[]{:S(2)}, u32[]{:S(2)}) %collective-permute-start.3) | collective-permute-done | bytes 3145760 | tf_op jit(solution)/shard_map/ppermute | solution.py:98
  148.8 6.5 convolution_convert_fusion.4
  162.5 4.1 constant_dynamic-update-slice_fusion.5
  169.7 7.5 convolution_convert_fusion.2
  182.1 7.2 convolution_convert_fusion.3
  189.5 42.0 %collective-permute-done.7 = bf16[768,2048]{1,0:T(8,128)(2,1)S(1)} collective-permute-done((bf16[768,2048]{1,0:T(8,128)(2,1)}, bf16[768,2048]{1,0:T(8,128)(2,1)S(1)}, u32[]{:S(2)}, u32[]{:S(2)}) %collective-permute-start.7) | collective-permute-done | bytes 3145760 | tf_op jit(solution)/shard_map/ppermute | solution.py:98
  231.5 6.2 convolution_convert_fusion.6
  242.6 13.1 %convolution_convert_fusion.1 = bf16[1536,2048]{1,0:T(8,128)(2,1)S(1)} fusion(bf16[3584,2048]{1,0:T(8,128)(2,1)} %param.9, s32[]{:T(128)S(6)} %select_n.2, bf16[1536,384]{0,1:T(8,128)(2,1)S(1)} %fusion.21, bf16[768,512]{0,1:T(8,128)(2,1)S(1)} %copy-done.44, bf16[768,512]{0,1:T(8,128)(2,1)S(1)} %copy-done.43), kind=kOutput, calls=%fused_computation.3 | convolution fusion | flops 5648547840 | bytes 12713988 | tf_op jit(solution)/shard_map/dot_general | solution.py:115
  256.2 8.1 convolution_convert_fusion.5
  273.6 6.0 fusion.26
  280.2 56.1 %collective-permute-done.10 = bf16[1536,1024]{0,1:T(8,128)(2,1)} collective-permute-done((bf16[1536,1024]{0,1:T(8,128)(2,1)S(1)}, bf16[1536,1024]{0,1:T(8,128)(2,1)}, u32[]{:S(2)}, u32[]{:S(2)}) %collective-permute-start.10) | collective-permute-done | bytes 3145760 | tf_op jit(solution)/shard_map/ppermute | solution.py:92
  340.1 7.3 add_convert_fusion.8.refs_0_
  349.0 5.1 convolution_convert_fusion.8
  354.0 5.1 convolution_convert_fusion.7
  359.2 27.7 %collective-permute-done.11 = bf16[1536,768]{0,1:T(8,128)(2,1)} collective-permute-done((bf16[1536,768]{0,1:T(8,128)(2,1)}, bf16[1536,768]{0,1:T(8,128)(2,1)}, u32[]{:S(2)}, u32[]{:S(2)}) %collective-permute-start.11) | collective-permute-done | bytes 2359328 | tf_op jit(solution)/shard_map/ppermute | solution.py:92
  392.4 28.2 %collective-permute-done.12 = bf16[1536,512]{0,1:T(8,128)(2,1)} collective-permute-done((bf16[1536,512]{0,1:T(8,128)(2,1)}, bf16[1536,512]{0,1:T(8,128)(2,1)}, u32[]{:S(2)}, u32[]{:S(2)}) %collective-permute-start.12) | collective-permute-done | bytes 1572896 | tf_op jit(solution)/shard_map/ppermute | solution.py:92
  420.6 5.0 fusion.52
  425.6 7.4 add_convert_fusion.11.refs_0_
  433.0 20.4 %collective-permute-done.14 = bf16[1536,512]{0,1:T(8,128)(2,1)} collective-permute-done((bf16[1536,512]{0,1:T(8,128)(2,1)}, bf16[1536,512]{0,1:T(8,128)(2,1)}, u32[]{:S(2)}, u32[]{:S(2)}) %collective-permute-start.14) | collective-permute-done | bytes 1572896 | tf_op jit(solution)/shard_map/ppermute | solution.py:92
  453.4 9.3 %convolution_convert_fusion = bf16[1536,2048]{1,0:T(8,128)(2,1)S(1)} fusion(bf16[1536,896]{0,1:T(8,128)(2,1)S(1)} %copy-done.22, bf16[3584,2048]{1,0:T(8,128)(2,1)} %param.9, s32[]{:T(128)S(6)} %select_n.2), kind=kOutput, calls=%fused_computation.2 | convolution fusion | flops 5640290304 | bytes 12713988 | tf_op jit(solution)/shard_map/dot_general | solution.py:115
  469.0 8.8 %collective-permute-done.16.refs_1_ = bf16[512,2048]{1,0:T(8,128)(2,1)} collective-permute-done((bf16[512,2048]{1,0:T(8,128)(2,1)S(1)}, bf16[512,2048]{1,0:T(8,128)(2,1)}, u32[]{:S(2)}, u32[]{:S(2)}) %collective-permute-start.16) | collective-permute-done | bytes 2097184 | tf_op jit(solution)/shard_map/ppermute | solution.py:95
  479.3 12.9 %shard_map.92.refs_4_ = bf16[3584,2048]{1,0:T(8,128)(2,1)} custom-call(s32[4]{0:T(128)S(1)} %pad_add_fusion.pos_ref, bf16[512,2048]{1,0:T(8,128)(2,1)S(1)} %add_convert_fusion.8.refs_0_, bf16[512,2048]{1,0:T(8,128)(2,1)} %collective-permute-done.16.refs_1_, bf16[512,2048]{1,0:T(8,128)(2,1)} %collective-permute-done.13.refs_2_, ...), custom_call_target="tpu_custom_call" | custom-call | bytes 16777216 | tf_op jit(solution)/shard_map/pallas_call | solution.py:68
  492.2 4.9 add_convert_fusion.4
  521.0 4.2 add_convert_fusion.7.refs_0_
  531.5 8.3 fusion.51
  539.8 11.2 %add_convert_fusion.1 = bf16[1536,2048]{1,0:T(8,128)(2,1)S(1)} fusion(f32[1536,2048]{1,0:T(8,128)} %fusion.51, bf16[1536,512]{0,1:T(8,128)(2,1)S(1)} %get-tuple-element.143, bf16[1536,512]{0,1:T(8,128)(2,1)S(1)} %get-tuple-element.144, bf16[2048,512]{1,0:T(8,128)(2,1)} %get-tuple-element.151, bf16[2048,512]{1,0:T(8,128)(2,1)} %get-tuple-element.152), kind=kOutput, calls=%fused_computation.1 | convolution fusion | flops 6463422464 | bytes 26214400 | tf_op jit(solution)/shard_map/dot_general | solution.py:20
  560.2 39.3 %collective-permute-done.20.refs_2_ = bf16[2048,512]{1,0:T(8,128)(2,1)} collective-permute-done((bf16[2048,512]{1,0:T(8,128)(2,1)S(1)}, bf16[2048,512]{1,0:T(8,128)(2,1)}, u32[]{:S(2)}, u32[]{:S(2)}) %collective-permute-start.20) | collective-permute-done | bytes 2097184 | tf_op jit(solution)/shard_map/ppermute | solution.py:98
  599.6 6.4 fusion.31
  606.0 7.9 add_convert_fusion.6.refs_0_
  621.6 8.2 fusion.50
  629.7 11.4 %add_convert_fusion = bf16[1536,2048]{1,0:T(8,128)(2,1)S(1)} fusion(f32[1536,2048]{1,0:T(8,128)} %fusion.50, bf16[1536,512]{0,1:T(8,128)(2,1)S(1)} %copy-done.11, bf16[1536,512]{0,1:T(8,128)(2,1)S(1)} %copy-done.13, bf16[2048,512]{1,0:T(8,128)(2,1)} %get-tuple-element.151, bf16[2048,512]{1,0:T(8,128)(2,1)} %get-tuple-element.152), kind=kOutput, calls=%fused_computation | convolution fusion | flops 6463422464 | bytes 26214400 | tf_op jit(solution)/shard_map/dot_general | solution.py:20
  644.2 8.2 collective-permute-done.27
  660.2 6.2 fusion.40
  666.5 4.7 add_convert_fusion.10.refs_0_
  671.1 5.6 fusion.37
  677.9 4.7 add_convert_fusion.9.refs_0_
  683.6 23.7 %collective-permute-done.34.refs_2_ = bf16[2048,512]{1,0:T(8,128)(2,1)} collective-permute-done((bf16[2048,512]{1,0:T(8,128)(2,1)S(1)}, bf16[2048,512]{1,0:T(8,128)(2,1)}, u32[]{:S(2)}, u32[]{:S(2)}) %collective-permute-start.34) | collective-permute-done | bytes 2097184 | tf_op jit(solution)/shard_map/ppermute | solution.py:98
  707.3 10.3 %shard_map.93 = bf16[3584,2048]{1,0:T(8,128)(2,1)} custom-call(s32[4]{0:T(128)S(1)} %pad_add_fusion.pos_ref, bf16[384,2048]{1,0:T(8,128)(2,1)} %add_convert_fusion.11.refs_0_, bf16[384,2048]{1,0:T(8,128)(2,1)} %collective-permute-done.22.refs_1_, bf16[384,2048]{1,0:T(8,128)(2,1)} %collective-permute-done.18.refs_2_, ...), custom_call_target="tpu_custom_call", output_to_operand_aliasing={{}: (5, {})} | custom-call | bytes 12582912 | tf_op jit(solution)/shard_map/pallas_call | solution.py:68
  717.6 13.1 %shard_map.94.refs_4_ = bf16[2048,3584]{1,0:T(8,128)(2,1)} custom-call(s32[4]{0:T(128)S(1)} %pad_add_fusion.pos_ref, bf16[2048,512]{1,0:T(8,128)(2,1)S(1)} %add_convert_fusion.7.refs_0_, bf16[2048,512]{1,0:T(8,128)(2,1)} %collective-permute-done.19.refs_1_, bf16[2048,512]{1,0:T(8,128)(2,1)} %collective-permute-done.20.refs_2_, ...), custom_call_target="tpu_custom_call" | custom-call | bytes 16777216 | tf_op jit(solution)/shard_map/pallas_call | solution.py:68
  732.2 8.8 %collective-permute-done.31.refs_2_ = bf16[2048,384]{1,0:T(8,128)(2,1)} collective-permute-done((bf16[2048,384]{1,0:T(8,128)(2,1)}, bf16[2048,384]{1,0:T(8,128)(2,1)}, u32[]{:S(2)}, u32[]{:S(2)}) %collective-permute-start.31) | collective-permute-done | bytes 1572896 | tf_op jit(solution)/shard_map/ppermute | solution.py:98
  742.8 47.9 %collective-permute-done.28 = bf16[192,2048]{1,0:T(8,128)(2,1)} collective-permute-done((bf16[192,2048]{1,0:T(8,128)(2,1)S(1)}, bf16[192,2048]{1,0:T(8,128)(2,1)}, u32[]{:S(2)}, u32[]{:S(2)}) %collective-permute-start.28) | collective-permute-done | bytes 786464 | tf_op jit(solution)/shard_map/ppermute | solution.py:98
  796.6 12.1 %shard_map.95.refs_4_ = bf16[2048,3584]{1,0:T(8,128)(2,1)} custom-call(s32[4]{0:T(128)S(1)} %pad_add_fusion.pos_ref, bf16[2048,512]{1,0:T(8,128)(2,1)S(1)} %copy-done.1, bf16[2048,512]{1,0:T(8,128)(2,1)S(1)} %copy-done.3, bf16[2048,512]{1,0:T(8,128)(2,1)} %collective-permute-done.34.refs_2_, bf16[2048,512]{1,0:T(8,128)(2,1)} %collective-permute-done.35.refs_3_), custom_call_target="tpu_custom_call" | custom-call | bytes 16777216 | tf_op jit(solution)/shard_map/pallas_call | solution.py:68
  808.8 10.3 %shard_map.96 = bf16[2048,3584]{1,0:T(8,128)(2,1)} custom-call(s32[4]{0:T(128)S(1)} %pad_add_fusion.pos_ref, bf16[2048,384]{1,0:T(8,128)(2,1)} %add_convert_fusion.10.refs_0_, bf16[2048,384]{1,0:T(8,128)(2,1)} %collective-permute-done.30.refs_1_, bf16[2048,384]{1,0:T(8,128)(2,1)} %collective-permute-done.31.refs_2_, ...), custom_call_target="tpu_custom_call", output_to_operand_aliasing={{}: (5, {})} | custom-call | bytes 12582912 | tf_op jit(solution)/shard_map/pallas_call | solution.py:68
  819.1 10.3 %shard_map.97 = bf16[2048,3584]{1,0:T(8,128)(2,1)} custom-call(s32[4]{0:T(128)S(1)} %pad_add_fusion.pos_ref, bf16[2048,384]{1,0:T(8,128)(2,1)} %add_convert_fusion.9.refs_0_, bf16[2048,384]{1,0:T(8,128)(2,1)} %collective-permute-done.36.refs_1_, bf16[2048,384]{1,0:T(8,128)(2,1)} %collective-permute-done.37.refs_2_, ...), custom_call_target="tpu_custom_call", output_to_operand_aliasing={{}: (5, {})} | custom-call | bytes 12582912 | tf_op jit(solution)/shard_map/pallas_call | solution.py:68
  (252 shorter events, 133.6 us)
Async XLA Ops:
  7.2 68.6 %all-gather.3.cloned.1.call-start = ((), (), s32[]{:S(2)}) async-start(), calls=%async_computation.4 | async-start | bytes 3932160 | tf_op jit(solution)/shard_map/all_gather | solution.py:145
  7.9 152.9 %all-gather.5.cloned.1.call-start = ((), (), s32[]{:S(2)}) async-start(), calls=%async_computation.5 | async-start | bytes 3932160 | tf_op jit(solution)/shard_map/all_gather | solution.py:146
  75.8 18.7 %collective-permute-start.1 = (bf16[768,2048]{1,0:T(8,128)(2,1)}, bf16[768,2048]{1,0:T(8,128)(2,1)}, u32[]{:S(2)}, u32[]{:S(2)}) collective-permute-start(bf16[768,2048]{1,0:T(8,128)(2,1)} %all-gather.3.cloned.1.call-done), channel_id=1, source_target_pairs={{0,8},{8,0},{16,24},{24,16},{1,9},{9,1},{17,25},{25,17},{2,10},{10... | collective-permute-start | bytes 9437192 | tf_op jit(solution)/shard_map/ppermute | solution.py:95
  75.8 70.7 %collective-permute-start.3 = (bf16[768,2048]{1,0:T(8,128)(2,1)}, bf16[768,2048]{1,0:T(8,128)(2,1)S(1)}, u32[]{:S(2)}, u32[]{:S(2)}) collective-permute-start(bf16[768,2048]{1,0:T(8,128)(2,1)} %all-gather.3.cloned.1.call-done), channel_id=1, source_target_pairs={{0,16},{8,24},{16,0},{24,8},{1,17},{9,25},{17,1},{25,9},{2,18},{10... | collective-permute-start | bytes 9437192 | tf_op jit(solution)/shard_map/ppermute | solution.py:98
  85.6 335.0 %reduce-scatter.5.cloned.1.call-start = ((), (), s32[]{:S(2)}) async-start(), calls=%async_computation.6 | async-start | bytes 3932160 | tf_op jit(solution)/shard_map/reduce_scatter | solution.py:138
  92.4 66.4 %copy-start.6 = (bf16[768,1024]{0,1:T(8,128)(2,1)}, bf16[768,1024]{0,1:T(8,128)(2,1)S(1)}, u32[]{:S(2)}) copy-start(bf16[768,1024]{0,1:T(8,128)(2,1)S(1)} %fusion.33) | copy-start | bytes 4718596
  92.5 64.3 %collective-permute-start = (bf16[768,1024]{0,1:T(8,128)(2,1)S(1)}, bf16[768,1024]{0,1:T(8,128)(2,1)S(1)}, u32[]{:S(2)}, u32[]{:S(2)}) collective-permute-start(bf16[768,1024]{0,1:T(8,128)(2,1)S(1)} %fusion.33), channel_id=1, source_target_pairs={{0,4},{4,0},{1,5},{5,1},{2,6},{6,2},{3,7},{7,3},{8,12},{12,8},{9,1... | collective-permute-start | bytes 4718600 | tf_op jit(solution)/shard_map/ppermute | solution.py:92
  102.2 75.1 %collective-permute-start.2 = (bf16[768,1024]{0,1:T(8,128)(2,1)}, bf16[768,1024]{0,1:T(8,128)(2,1)}, u32[]{:S(2)}, u32[]{:S(2)}) collective-permute-start(bf16[768,1024]{0,1:T(8,128)(2,1)} %convolution_convert_fusion.9), channel_id=1, source_target_pairs={{0,4},{4,0},{1,5},{5,1},{2,6},{6,2},{3,7},{7,3},{8,12},{12,8},{9,1... | collective-permute-start | bytes 4718600 | tf_op jit(solution)/shard_map/ppermute | solution.py:92
  146.5 20.1 %collective-permute-start.4 = (bf16[768,2048]{1,0:T(8,128)(2,1)S(1)}, bf16[768,2048]{1,0:T(8,128)(2,1)}, u32[]{:S(2)}, u32[]{:S(2)}) collective-permute-start(bf16[768,2048]{1,0:T(8,128)(2,1)S(1)} %collective-permute-done.3), channel_id=1, source_target_pairs={{0,8},{8,0},{16,24},{24,16},{1,9},{9,1},{17,25},{25,17},{2,10},{10... | collective-permute-start | bytes 9437192 | tf_op jit(solution)/shard_map/ppermute | solution.py:95
  155.3 82.4 %collective-permute-start.5 = (bf16[1536,768]{0,1:T(8,128)(2,1)}, bf16[1536,768]{0,1:T(8,128)(2,1)}, u32[]{:S(2)}, u32[]{:S(2)}) collective-permute-start(bf16[1536,768]{0,1:T(8,128)(2,1)} %convolution_convert_fusion.4), channel_id=1, source_target_pairs={{0,4},{4,0},{1,5},{5,1},{2,6},{6,2},{3,7},{7,3},{8,12},{12,8},{9,1... | collective-permute-start | bytes 7077896 | tf_op jit(solution)/shard_map/ppermute | solution.py:92
  160.8 28.5 %collective-permute-start.6 = (bf16[768,2048]{1,0:T(8,128)(2,1)}, bf16[768,2048]{1,0:T(8,128)(2,1)S(1)}, u32[]{:S(2)}, u32[]{:S(2)}) collective-permute-start(bf16[768,2048]{1,0:T(8,128)(2,1)} %all-gather.5.cloned.1.call-done), channel_id=1, source_target_pairs={{0,8},{8,0},{16,24},{24,16},{1,9},{9,1},{17,25},{25,17},{2,10},{10... | collective-permute-start | bytes 9437192 | tf_op jit(solution)/shard_map/ppermute | solution.py:95
  161.0 70.5 %collective-permute-start.7 = (bf16[768,2048]{1,0:T(8,128)(2,1)}, bf16[768,2048]{1,0:T(8,128)(2,1)S(1)}, u32[]{:S(2)}, u32[]{:S(2)}) collective-permute-start(bf16[768,2048]{1,0:T(8,128)(2,1)} %all-gather.5.cloned.1.call-done), channel_id=1, source_target_pairs={{0,16},{8,24},{16,0},{24,8},{1,17},{9,25},{17,1},{25,9},{2,18},{10... | collective-permute-start | bytes 9437192 | tf_op jit(solution)/shard_map/ppermute | solution.py:98
  177.3 159.0 %copy-start.4 = (bf16[1536,1024]{0,1:T(8,128)(2,1)}, bf16[1536,1024]{0,1:T(8,128)(2,1)S(1)}, u32[]{:S(2)}) copy-start(bf16[1536,1024]{0,1:T(8,128)(2,1)S(1)} %convolution_convert_fusion.2) | copy-start | bytes 9437188
  231.5 24.2 %collective-permute-start.8 = (bf16[768,2048]{1,0:T(8,128)(2,1)S(1)}, bf16[768,2048]{1,0:T(8,128)(2,1)S(1)}, u32[]{:S(2)}, u32[]{:S(2)}) collective-permute-start(bf16[768,2048]{1,0:T(8,128)(2,1)S(1)} %collective-permute-done.7), channel_id=1, source_target_pairs={{0,8},{8,0},{16,24},{24,16},{1,9},{9,1},{17,25},{25,17},{2,10},{10... | collective-permute-start | bytes 9437192 | tf_op jit(solution)/shard_map/ppermute | solution.py:95
  264.7 5.8 collective-permute-start.9
  265.2 71.1 %collective-permute-start.10 = (bf16[1536,1024]{0,1:T(8,128)(2,1)S(1)}, bf16[1536,1024]{0,1:T(8,128)(2,1)}, u32[]{:S(2)}, u32[]{:S(2)}) collective-permute-start(bf16[1536,1024]{0,1:T(8,128)(2,1)S(1)} %convolution_convert_fusion.2), channel_id=1, source_target_pairs={{0,4},{4,0},{1,5},{5,1},{2,6},{6,2},{3,7},{7,3},{8,12},{12,8},{9,1... | collective-permute-start | bytes 9437192 | tf_op jit(solution)/shard_map/ppermute | solution.py:92
  265.8 121.1 %collective-permute-start.11 = (bf16[1536,768]{0,1:T(8,128)(2,1)}, bf16[1536,768]{0,1:T(8,128)(2,1)}, u32[]{:S(2)}, u32[]{:S(2)}) collective-permute-start(bf16[1536,768]{0,1:T(8,128)(2,1)} %convolution_convert_fusion.3), channel_id=1, source_target_pairs={{0,4},{4,0},{1,5},{5,1},{2,6},{6,2},{3,7},{7,3},{8,12},{12,8},{9,1... | collective-permute-start | bytes 7077896 | tf_op jit(solution)/shard_map/ppermute | solution.py:92
  267.3 153.3 %collective-permute-start.12 = (bf16[1536,512]{0,1:T(8,128)(2,1)}, bf16[1536,512]{0,1:T(8,128)(2,1)}, u32[]{:S(2)}, u32[]{:S(2)}) collective-permute-start(bf16[1536,512]{0,1:T(8,128)(2,1)} %convolution_convert_fusion.6), channel_id=1, source_target_pairs={{0,4},{4,0},{1,5},{5,1},{2,6},{6,2},{3,7},{7,3},{8,12},{12,8},{9,1... | collective-permute-start | bytes 4718600 | tf_op jit(solution)/shard_map/ppermute | solution.py:92
  273.6 326.0 %reduce-scatter.7.cloned.1.call-start = ((), (), s32[]{:S(2)}) async-start(), calls=%async_computation.7 | async-start | bytes 3932160 | tf_op jit(solution)/shard_map/reduce_scatter | solution.py:138
  279.6 173.8 %collective-permute-start.14 = (bf16[1536,512]{0,1:T(8,128)(2,1)}, bf16[1536,512]{0,1:T(8,128)(2,1)}, u32[]{:S(2)}, u32[]{:S(2)}) collective-permute-start(bf16[1536,512]{0,1:T(8,128)(2,1)} %convolution_convert_fusion.5), channel_id=1, source_target_pairs={{0,4},{4,0},{1,5},{5,1},{2,6},{6,2},{3,7},{7,3},{8,12},{12,8},{9,1... | collective-permute-start | bytes 4718600 | tf_op jit(solution)/shard_map/ppermute | solution.py:92
  347.4 106.0 %collective-permute-start.13 = (bf16[512,2048]{1,0:T(8,128)(2,1)S(1)}, bf16[512,2048]{1,0:T(8,128)(2,1)}, u32[]{:S(2)}, u32[]{:S(2)}) collective-permute-start(bf16[512,2048]{1,0:T(8,128)(2,1)S(1)} %add_convert_fusion.8.refs_0_), channel_id=1, source_target_pairs={{0,16},{8,24},{16,0},{24,8},{1,17},{9,25},{17,1},{25,9},{2,18},{10... | collective-permute-start | bytes 6291464 | tf_op jit(solution)/shard_map/ppermute | solution.py:98
  466.4 25.8 %collective-permute-start.15 = (bf16[768,2048]{1,0:T(8,128)(2,1)}, bf16[768,2048]{1,0:T(8,128)(2,1)}, u32[]{:S(2)}, u32[]{:S(2)}) collective-permute-start(bf16[768,2048]{1,0:T(8,128)(2,1)} %slice.163), channel_id=1, source_target_pairs={{0,8},{8,0},{16,24},{24,16},{1,9},{9,1},{17,25},{25,17},{2,10},{10... | collective-permute-start | bytes 9437192 | tf_op jit(solution)/shard_map/ppermute | solution.py:95
  466.4 11.4 %collective-permute-start.16 = (bf16[512,2048]{1,0:T(8,128)(2,1)S(1)}, bf16[512,2048]{1,0:T(8,128)(2,1)}, u32[]{:S(2)}, u32[]{:S(2)}) collective-permute-start(bf16[512,2048]{1,0:T(8,128)(2,1)S(1)} %add_convert_fusion.8.refs_0_), channel_id=1, source_target_pairs={{0,8},{8,0},{16,24},{24,16},{1,9},{9,1},{17,25},{25,17},{2,10},{10... | collective-permute-start | bytes 6291464 | tf_op jit(solution)/shard_map/ppermute | solution.py:95
  466.9 12.4 %collective-permute-start.17 = (bf16[512,2048]{1,0:T(8,128)(2,1)}, bf16[512,2048]{1,0:T(8,128)(2,1)}, u32[]{:S(2)}, u32[]{:S(2)}) collective-permute-start(bf16[512,2048]{1,0:T(8,128)(2,1)} %collective-permute-done.13.refs_2_), channel_id=1, source_target_pairs={{0,8},{8,0},{16,24},{24,16},{1,9},{9,1},{17,25},{25,17},{2,10},{10... | collective-permute-start | bytes 6291464 | tf_op jit(solution)/shard_map/ppermute | solution.py:95
  467.0 58.3 %collective-permute-start.24 = (bf16[1536,384]{0,1:T(8,128)(2,1)}, bf16[1536,384]{0,1:T(8,128)(2,1)}, u32[]{:S(2)}, u32[]{:S(2)}) collective-permute-start(bf16[1536,384]{0,1:T(8,128)(2,1)} %convolution_convert_fusion.7), channel_id=1, source_target_pairs={{0,4},{4,0},{1,5},{5,1},{2,6},{6,2},{3,7},{7,3},{8,12},{12,8},{9,1... | collective-permute-start | bytes 3538952 | tf_op jit(solution)/shard_map/ppermute | solution.py:92
  467.6 57.8 %collective-permute-start.25 = (bf16[1536,384]{0,1:T(8,128)(2,1)}, bf16[1536,384]{0,1:T(8,128)(2,1)}, u32[]{:S(2)}, u32[]{:S(2)}) collective-permute-start(bf16[1536,384]{0,1:T(8,128)(2,1)} %convolution_convert_fusion.8), channel_id=1, source_target_pairs={{0,4},{4,0},{1,5},{5,1},{2,6},{6,2},{3,7},{7,3},{8,12},{12,8},{9,1... | collective-permute-start | bytes 3538952 | tf_op jit(solution)/shard_map/ppermute | solution.py:92
  477.8 37.0 %collective-permute-start.18 = (bf16[384,2048]{1,0:T(8,128)(2,1)}, bf16[384,2048]{1,0:T(8,128)(2,1)}, u32[]{:S(2)}, u32[]{:S(2)}) collective-permute-start(bf16[384,2048]{1,0:T(8,128)(2,1)} %add_convert_fusion.11.refs_0_), channel_id=1, source_target_pairs={{0,16},{8,24},{16,0},{24,8},{1,17},{9,25},{17,1},{25,9},{2,18},{10... | collective-permute-start | bytes 4718600 | tf_op jit(solution)/shard_map/ppermute | solution.py:98
  497.1 294.2 %reduce-scatter.11.cloned.1.call-start = ((), (), s32[]{:S(2)}) async-start(), calls=%async_computation.9 | async-start | bytes 3932160 | tf_op jit(solution)/shard_map/reduce_scatter | solution.py:138
  551.3 5.7 collective-permute-start.26
  551.4 48.2 %collective-permute-start.20 = (bf16[2048,512]{1,0:T(8,128)(2,1)S(1)}, bf16[2048,512]{1,0:T(8,128)(2,1)}, u32[]{:S(2)}, u32[]{:S(2)}) collective-permute-start(bf16[2048,512]{1,0:T(8,128)(2,1)S(1)} %add_convert_fusion.7.refs_0_), channel_id=1, source_target_pairs={{0,16},{8,24},{16,0},{24,8},{1,17},{9,25},{17,1},{25,9},{2,18},{10... | collective-permute-start | bytes 6291464 | tf_op jit(solution)/shard_map/ppermute | solution.py:98
  560.2 269.2 %reduce-scatter.9.cloned.1.call-start = ((), (), s32[]{:S(2)}) async-start(), calls=%async_computation.8 | async-start | bytes 3932160 | tf_op jit(solution)/shard_map/reduce_scatter | solution.py:138
  641.5 10.9 %collective-permute-start.27 = (bf16[768,2048]{1,0:T(8,128)(2,1)S(1)}, bf16[768,2048]{1,0:T(8,128)(2,1)S(1)}, u32[]{:S(2)}, u32[]{:S(2)}) collective-permute-start(bf16[768,2048]{1,0:T(8,128)(2,1)S(1)} %slice.175), channel_id=1, source_target_pairs={{0,8},{8,0},{16,24},{24,16},{1,9},{9,1},{17,25},{25,17},{2,10},{10... | collective-permute-start | bytes 9437192 | tf_op jit(solution)/shard_map/ppermute | solution.py:95
  641.6 35.2 %collective-permute-start.22 = (bf16[384,2048]{1,0:T(8,128)(2,1)}, bf16[384,2048]{1,0:T(8,128)(2,1)}, u32[]{:S(2)}, u32[]{:S(2)}) collective-permute-start(bf16[384,2048]{1,0:T(8,128)(2,1)} %add_convert_fusion.11.refs_0_), channel_id=1, source_target_pairs={{0,8},{8,0},{16,24},{24,16},{1,9},{9,1},{17,25},{25,17},{2,10},{10... | collective-permute-start | bytes 4718600 | tf_op jit(solution)/shard_map/ppermute | solution.py:95
  642.1 34.8 %collective-permute-start.23 = (bf16[384,2048]{1,0:T(8,128)(2,1)}, bf16[384,2048]{1,0:T(8,128)(2,1)}, u32[]{:S(2)}, u32[]{:S(2)}) collective-permute-start(bf16[384,2048]{1,0:T(8,128)(2,1)} %collective-permute-done.18.refs_2_), channel_id=1, source_target_pairs={{0,8},{8,0},{16,24},{24,16},{1,9},{9,1},{17,25},{25,17},{2,10},{10... | collective-permute-start | bytes 4718600 | tf_op jit(solution)/shard_map/ppermute | solution.py:95
  642.1 40.5 %collective-permute-start.19 = (bf16[2048,512]{1,0:T(8,128)(2,1)S(1)}, bf16[2048,512]{1,0:T(8,128)(2,1)}, u32[]{:S(2)}, u32[]{:S(2)}) collective-permute-start(bf16[2048,512]{1,0:T(8,128)(2,1)S(1)} %add_convert_fusion.7.refs_0_), channel_id=1, source_target_pairs={{0,8},{8,0},{16,24},{24,16},{1,9},{9,1},{17,25},{25,17},{2,10},{10... | collective-permute-start | bytes 6291464 | tf_op jit(solution)/shard_map/ppermute | solution.py:95
  644.1 73.4 %collective-permute-start.21 = (bf16[2048,512]{1,0:T(8,128)(2,1)}, bf16[2048,512]{1,0:T(8,128)(2,1)}, u32[]{:S(2)}, u32[]{:S(2)}) collective-permute-start(bf16[2048,512]{1,0:T(8,128)(2,1)} %collective-permute-done.20.refs_2_), channel_id=1, source_target_pairs={{0,8},{8,0},{16,24},{24,16},{1,9},{9,1},{17,25},{25,17},{2,10},{10... | collective-permute-start | bytes 6291464 | tf_op jit(solution)/shard_map/ppermute | solution.py:95
  658.7 48.6 %collective-permute-start.34 = (bf16[2048,512]{1,0:T(8,128)(2,1)S(1)}, bf16[2048,512]{1,0:T(8,128)(2,1)}, u32[]{:S(2)}, u32[]{:S(2)}) collective-permute-start(bf16[2048,512]{1,0:T(8,128)(2,1)S(1)} %copy-done), channel_id=1, source_target_pairs={{0,16},{8,24},{16,0},{24,8},{1,17},{9,25},{17,1},{25,9},{2,18},{10... | collective-permute-start | bytes 6291464 | tf_op jit(solution)/shard_map/ppermute | solution.py:98
  676.8 64.2 %collective-permute-start.33 = (bf16[2048,512]{1,0:T(8,128)(2,1)S(1)}, bf16[2048,512]{1,0:T(8,128)(2,1)S(1)}, u32[]{:S(2)}, u32[]{:S(2)}) collective-permute-start(bf16[2048,512]{1,0:T(8,128)(2,1)S(1)} %copy-done), channel_id=1, source_target_pairs={{0,8},{8,0},{16,24},{24,16},{1,9},{9,1},{17,25},{25,17},{2,10},{10... | collective-permute-start | bytes 6291464 | tf_op jit(solution)/shard_map/ppermute | solution.py:95
  676.9 64.1 %collective-permute-start.31 = (bf16[2048,384]{1,0:T(8,128)(2,1)}, bf16[2048,384]{1,0:T(8,128)(2,1)}, u32[]{:S(2)}, u32[]{:S(2)}) collective-permute-start(bf16[2048,384]{1,0:T(8,128)(2,1)} %add_convert_fusion.10.refs_0_), channel_id=1, source_target_pairs={{0,16},{8,24},{16,0},{24,8},{1,17},{9,25},{17,1},{25,9},{2,18},{10... | collective-permute-start | bytes 4718600 | tf_op jit(solution)/shard_map/ppermute | solution.py:98
  682.6 108.1 %collective-permute-start.37 = (bf16[2048,384]{1,0:T(8,128)(2,1)}, bf16[2048,384]{1,0:T(8,128)(2,1)}, u32[]{:S(2)}, u32[]{:S(2)}) collective-permute-start(bf16[2048,384]{1,0:T(8,128)(2,1)} %add_convert_fusion.9.refs_0_), channel_id=1, source_target_pairs={{0,16},{8,24},{16,0},{24,8},{1,17},{9,25},{17,1},{25,9},{2,18},{10... | collective-permute-start | bytes 4718600 | tf_op jit(solution)/shard_map/ppermute | solution.py:98
  707.3 84.0 %collective-permute-start.35 = (bf16[2048,512]{1,0:T(8,128)(2,1)}, bf16[2048,512]{1,0:T(8,128)(2,1)}, u32[]{:S(2)}, u32[]{:S(2)}) collective-permute-start(bf16[2048,512]{1,0:T(8,128)(2,1)} %collective-permute-done.34.refs_2_), channel_id=1, source_target_pairs={{0,8},{8,0},{16,24},{24,16},{1,9},{9,1},{17,25},{25,17},{2,10},{10... | collective-permute-start | bytes 6291464 | tf_op jit(solution)/shard_map/ppermute | solution.py:95
  717.6 75.2 %copy-start.42 = (bf16[192,2048]{1,0:T(8,128)(2,1)S(1)}, bf16[192,2048]{1,0:T(8,128)(2,1)}, u32[]{:S(2)}) copy-start(bf16[192,2048]{1,0:T(8,128)(2,1)} %reduce-scatter.5.cloned.1.call-done) | copy-start | bytes 2359300
  730.7 60.1 %collective-permute-start.28 = (bf16[192,2048]{1,0:T(8,128)(2,1)S(1)}, bf16[192,2048]{1,0:T(8,128)(2,1)}, u32[]{:S(2)}, u32[]{:S(2)}) collective-permute-start(bf16[192,2048]{1,0:T(8,128)(2,1)S(1)} %copy-done.45), channel_id=1, source_target_pairs={{0,16},{8,24},{16,0},{24,8},{1,17},{9,25},{17,1},{25,9},{2,18},{10... | collective-permute-start | bytes 2359304 | tf_op jit(solution)/shard_map/ppermute | solution.py:98
  741.0 67.8 %collective-permute-start.30 = (bf16[2048,384]{1,0:T(8,128)(2,1)}, bf16[2048,384]{1,0:T(8,128)(2,1)}, u32[]{:S(2)}, u32[]{:S(2)}) collective-permute-start(bf16[2048,384]{1,0:T(8,128)(2,1)} %add_convert_fusion.10.refs_0_), channel_id=1, source_target_pairs={{0,8},{8,0},{16,24},{24,16},{1,9},{9,1},{17,25},{25,17},{2,10},{10... | collective-permute-start | bytes 4718600 | tf_op jit(solution)/shard_map/ppermute | solution.py:95
  742.3 66.5 %collective-permute-start.32 = (bf16[2048,384]{1,0:T(8,128)(2,1)}, bf16[2048,384]{1,0:T(8,128)(2,1)}, u32[]{:S(2)}, u32[]{:S(2)}) collective-permute-start(bf16[2048,384]{1,0:T(8,128)(2,1)} %collective-permute-done.31.refs_2_), channel_id=1, source_target_pairs={{0,8},{8,0},{16,24},{24,16},{1,9},{9,1},{17,25},{25,17},{2,10},{10... | collective-permute-start | bytes 4718600 | tf_op jit(solution)/shard_map/ppermute | solution.py:95
  790.7 28.3 %collective-permute-start.36 = (bf16[2048,384]{1,0:T(8,128)(2,1)}, bf16[2048,384]{1,0:T(8,128)(2,1)}, u32[]{:S(2)}, u32[]{:S(2)}) collective-permute-start(bf16[2048,384]{1,0:T(8,128)(2,1)} %add_convert_fusion.9.refs_0_), channel_id=1, source_target_pairs={{0,8},{8,0},{16,24},{24,16},{1,9},{9,1},{17,25},{25,17},{2,10},{10... | collective-permute-start | bytes 4718600 | tf_op jit(solution)/shard_map/ppermute | solution.py:95
  790.8 28.3 %collective-permute-start.38 = (bf16[2048,384]{1,0:T(8,128)(2,1)}, bf16[2048,384]{1,0:T(8,128)(2,1)}, u32[]{:S(2)}, u32[]{:S(2)}) collective-permute-start(bf16[2048,384]{1,0:T(8,128)(2,1)} %collective-permute-done.37.refs_2_), channel_id=1, source_target_pairs={{0,8},{8,0},{16,24},{24,16},{1,9},{9,1},{17,25},{25,17},{2,10},{10... | collective-permute-start | bytes 4718600 | tf_op jit(solution)/shard_map/ppermute | solution.py:95
  791.3 38.1 %collective-permute-start.29 = (bf16[192,2048]{1,0:T(8,128)(2,1)}, bf16[192,2048]{1,0:T(8,128)(2,1)}, u32[]{:S(2)}, u32[]{:S(2)}) collective-permute-start(bf16[192,2048]{1,0:T(8,128)(2,1)} %reduce-scatter.11.cloned.1.call-done), channel_id=1, source_target_pairs={{0,16},{8,24},{16,0},{24,8},{1,17},{9,25},{17,1},{25,9},{2,18},{10... | collective-permute-start | bytes 2359304 | tf_op jit(solution)/shard_map/ppermute | solution.py:98
  (57 other events, 564.5 us)
Sparse Core Ops, SparseCore 0:
  9.6 66.1 all-gather.2
  85.7 61.2 all-gather.4
  273.7 58.0 reduce-scatter.4
  497.2 57.1 reduce-scatter.6
  560.3 57.9 reduce-scatter.10
  655.6 58.0 reduce-scatter.8
